TPU v7x, 32 devices: a whole 2x2x4 slice. The times are simulated.
32 devices in a mesh: tile: 8 (over z, x), mem: 4 (over y, core).
Axes of the slice: x: 2, y: 2, z: 4, core: 2. Of those that a mesh axis runs over, the one named last changes fastest.
Arguments:
- control: float32 [64, 64, 4096], P('mem', None, 'tile'), may hold values from -8 to 8
- ensemble: bfloat16 [64, 5, 64, 4096], P('mem', None, None, 'tile'), may hold values from -6 to 6
- jacobian: bfloat16 [640, 320], replicated, may hold values from -0.3125 to 0.3125
- send_columns: int32 [32, 8, 2], P(('tile', 'mem')), may hold values from 0 to 127, as said below
- received_counts: int32 [32, 8], P(('tile', 'mem')), may hold values from 0 to 2, as said below
- observed_channel: int32 [32, 8, 2, 128], P(('tile', 'mem')), may hold values from 0 to 639
- innovation: float32 [32, 8, 2, 128], P(('tile', 'mem')), may hold values from -1.5 to 1.5
- error_weight: float32 [32, 8, 2, 128], P(('tile', 'mem')), may hold values from 1 to 10
Outputs:
- gradient: float32 [64, 64, 4096], P('mem', None, 'tile')
- departures: float32 [32, 8, 2, 128], P(('tile', 'mem'))
Inputs may be any that keep to these rules, and one draw needn't show every extreme that they name: `send_columns`: entry [d, t, j] is a column within the 128 columns of block k of strip s, where d = s * 4 + k; the entries of one row d are distinct. `received_counts`: entry [e, s] counts the used slots, from the first, of the 2 slots that device e receives from tile s. In each mem group one owner receives 2 from every source tile.
All inputs are finite; a program needn't handle non-finite values.
Results may differ from a plain program's by a relative error of at most 0.01.
Values may be sent and summed in bfloat16 or wider, within the bound.
A program may use at most 64 MiB of HBM per device.

v0:
```python
import math

import jax
import jax.numpy as jnp
from jax import lax
from jax.sharding import PartitionSpec as P

NY = 64


diffusion_coef = 0.2


def extended_2(block, sides, width):
    for axis, dim in sides:
        count = lax.axis_size(axis)
        forward = [(i, i + 1) for i in range(count - 1)]
        backward = [(target, source) for source, target in forward]
        low = lax.ppermute(
            lax.slice_in_dim(block, block.shape[dim] - width, None, axis=dim), axis, forward
        )
        high = lax.ppermute(lax.slice_in_dim(block, 0, width, axis=dim), axis, backward)
        block = jnp.concatenate([low, block, high], axis=dim)
    return block


def y_neighbours(state_field):
    length = state_field.shape[-1]
    position = lax.iota(jnp.int32, length) % NY
    zeros_edge = jnp.zeros(state_field.shape[:-1] + (1,), state_field.dtype)
    upward = jnp.concatenate([state_field[..., 1:], zeros_edge], -1)
    downward = jnp.concatenate([zeros_edge, state_field[..., :-1]], -1)
    return jnp.where(position == NY - 1, 0.0, upward) + jnp.where(position == 0, 0.0, downward)


def widen_with_halo(state_field):
    return extended_2(state_field, (("tile", 2),), 4 * NY)


def localize(state_field, tile_index, strip_rows, grid_rows):
    halo_depth = 4
    extended = widen_with_halo(state_field)
    for inner_step in range(halo_depth):
        middle = extended[..., NY:-NY]
        swept = middle + diffusion_coef * (
            extended[..., : -2 * NY] + extended[..., 2 * NY :] + y_neighbours(middle) - 4.0 * middle
        )
        first_row = tile_index * strip_rows - (halo_depth - 1 - inner_step)
        domain_wide_row = first_row + lax.iota(jnp.int32, swept.shape[-1]) // NY
        extended = jnp.where((domain_wide_row >= 0) & (domain_wide_row < grid_rows), swept, 0.0)
    return extended


def pick_channels(block):
    model_block, channel_block = block
    channel_ids = lax.iota(jnp.int32, model_block.shape[-1])
    hits = channel_block[:, :, None] == channel_ids[None, None, :]
    return jnp.sum(jnp.where(hits, model_block[:, None, :], 0.0), axis=2)


def spread_channels(block):
    weighted_block, channel_block, channel_count = (block[0], block[1], block[2].shape[-1])
    channel_ids = lax.iota(jnp.int32, channel_count)
    hits = channel_block[:, :, None] == channel_ids[None, None, :]
    return jnp.sum(jnp.where(hits, weighted_block[:, :, None], 0.0), axis=1)


def body(
    control,
    ensemble,
    jacobian,
    send_columns,
    received_counts,
    observed_channel,
    innovation,
    error_weight,
):
    members = control.shape[0] * lax.axis_size("mem")
    member_scale = 1.0 / math.sqrt(members)
    tile_columns = control.shape[2]
    strip_rows = tile_columns // NY
    grid_rows = strip_rows * lax.axis_size("tile")
    tile_index = lax.axis_index("tile")
    state_size = ensemble.shape[1] * ensemble.shape[2]
    channels = jacobian.shape[0]
    localized_member_field = localize(control, tile_index, strip_rows, grid_rows)
    localization_weights = localized_member_field.astype(jnp.bfloat16)
    member_sum = (
        jnp.einsum(
            "teb,tqeb->qeb", localization_weights, ensemble, preferred_element_type=jnp.float32
        )
        * member_scale
    )
    member_sum = member_sum.reshape(state_size, tile_columns)
    block_sum = lax.psum_scatter(member_sum, "mem", scatter_dimension=1, tiled=True).astype(
        jnp.bfloat16
    )
    block_columns = block_sum.shape[1]
    slot_table = send_columns[0]
    owner_count = slot_table.shape[0]
    count_of_slots = slot_table.shape[1]
    row_count = owner_count * count_of_slots
    slot_hits = (
        slot_table.reshape(row_count, 1) == lax.iota(jnp.int32, block_columns)[None, :]
    ).astype(jnp.bfloat16)
    outgoing = jnp.einsum(
        "sc,ic->si", slot_hits, block_sum, preferred_element_type=jnp.float32
    ).astype(jnp.bfloat16)
    incoming = lax.all_to_all(
        outgoing.reshape(owner_count, count_of_slots, state_size),
        "tile",
        split_axis=0,
        concat_axis=0,
        tiled=True,
    )
    model_channels = jnp.dot(
        incoming.reshape(row_count, state_size),
        jnp.transpose(jacobian),
        preferred_element_type=jnp.float32,
    )
    observed_count = observed_channel.shape[-1]
    channel_rows = observed_channel[0].reshape(row_count, observed_count)
    block_count = math.gcd(row_count, 8)
    block_rows = row_count // block_count
    evolved = lax.map(
        pick_channels,
        (
            model_channels.reshape(block_count, block_rows, channels),
            channel_rows.reshape(block_count, block_rows, observed_count),
        ),
    )
    evolved = evolved.reshape(owner_count, count_of_slots, observed_count)
    filled = (
        jnp.arange(count_of_slots, dtype=jnp.int32)[None, :, None]
        < received_counts[0][:, None, None]
    )
    departures = jnp.where(filled, evolved - innovation[0], 0.0)
    weighted = error_weight[0] * departures
    channel_shape = jnp.zeros((block_count, channels), jnp.int32)
    channel_adjoint = lax.map(
        spread_channels,
        (
            weighted.reshape(block_count, block_rows, observed_count),
            channel_rows.reshape(block_count, block_rows, observed_count),
            channel_shape,
        ),
    )
    channel_adjoint = channel_adjoint.reshape(row_count, channels)
    column_adjoint = jnp.dot(
        channel_adjoint.astype(jnp.bfloat16), jacobian, preferred_element_type=jnp.float32
    ).astype(jnp.bfloat16)
    returned = lax.all_to_all(
        column_adjoint.reshape(owner_count, count_of_slots, state_size),
        "tile",
        split_axis=0,
        concat_axis=0,
        tiled=True,
    )
    block_adjoint = jnp.einsum(
        "si,sc->ic",
        returned.reshape(row_count, state_size),
        slot_hits,
        preferred_element_type=jnp.float32,
    ).astype(jnp.bfloat16)
    strip_adjoint = lax.all_gather(block_adjoint, "mem", axis=1, tiled=True)
    analysis_increment_adjoint = strip_adjoint.reshape(
        ensemble.shape[1], ensemble.shape[2], tile_columns
    )
    member_adjoint = (
        jnp.einsum(
            "roug,oug->rug",
            ensemble,
            analysis_increment_adjoint,
            preferred_element_type=jnp.float32,
        )
        * member_scale
    )
    gradient = localize(member_adjoint, tile_index, strip_rows, grid_rows)
    return (gradient, departures[None])


def solution(mesh):
    in_specs = (
        P("mem", None, "tile"),
        P("mem", None, None, "tile"),
        P(),
        P(("tile", "mem"), None, None),
        P(("tile", "mem"), None),
        P(("tile", "mem"), None, None, None),
        P(("tile", "mem"), None, None, None),
        P(("tile", "mem"), None, None, None),
    )
    out_specs = (P("mem", None, "tile"), P(("tile", "mem"), None, None, None))
    return jax.shard_map(body, mesh=mesh, in_specs=in_specs, out_specs=out_specs, check_vma=False)
```

profile of v0, /device:TPU:0, one launch (start us, length us, event | category | flops | bytes accessed | tf_op | source)
XLA Modules:
  0.0 221.4 jit_solution(18232815243879671937)
XLA Ops:
  7.2 3.3 %fusion.105 = (f32[16,64,256]{2,1,0:T(8,128)}, f32[16,64,256]{2,1,0:T(8,128)}) fusion(f32[16,64,512]{2,1,0:T(8,128)} %param.12), kind=kLoop, calls=%fused_computation.159 | loop fusion | bytes 4194304 | tf_op jit(solution)/shard_map/slice | solution.py:22
  10.5 5.8 %collective-permute-start = (f32[16,64,256]{2,1,0:T(8,128)}, f32[16,64,256]{2,1,0:T(8,128)}, u32[]{:S(2)}, u32[]{:S(2)}) collective-permute-start(f32[16,64,256]{2,1,0:T(8,128)} %get-tuple-element.99), channel_id=1, source_target_pairs={{0,4},{4,8},{8,12},{12,16},{16,20},{20,24},{24,28},{1,5},{5,9},{9,... | collective-permute-start | bytes 3145736 | tf_op jit(solution)/shard_map/ppermute | solution.py:19
  16.3 1.3 collective-permute-start.1
  17.9 42.7 %collective-permute-done = f32[16,64,256]{2,1,0:T(8,128)} collective-permute-done((f32[16,64,256]{2,1,0:T(8,128)}, f32[16,64,256]{2,1,0:T(8,128)}, u32[]{:S(2)}, u32[]{:S(2)}) %collective-permute-start) | collective-permute-done | bytes 1048608 | tf_op jit(solution)/shard_map/ppermute | solution.py:19
  60.5 1.4 constant_dynamic-update-slice_fusion.2
  62.3 2.0 fusion.97
  64.3 2.5 %fusion.9 = f32[16,64,896]{2,1,0:T(8,128)S(1)} fusion(f32[16,64,1024]{2,1,0:T(8,128)S(1)} %constant_dynamic-update-slice_fusion, f32[16,64,895]{2,1,0:T(8,128)S(1)} %get-tuple-element.83, f32[16,64,895]{2,1,0:T(8,128)S(1)} %get-tuple-element.82, pred[896]{0:T(1024)(128)(4,1)S(1)} %get-tuple-element.102, pred[896]{0:T(1024)(128)(4,1)S(1)} %get-tuple-element.103, ...), kind=kLoop, calls=%fused_computation.25 | loop fusion | flops 9175040 | bytes 22014592 | tf_op jit(solution)/shard_map/jit(_where)/select_n | solution.py:50
  66.7 1.7 fusion.99
  68.4 2.0 fusion.19
  70.4 1.4 fusion.101
  71.9 1.4 fusion.29
  73.3 1.1 fusion.103
  74.5 1.2 bitcast_convert_fusion
  76.0 1.1 multiply_reduce_fusion.1
  77.1 0.9 broadcast_multiply_fusion
  78.2 23.7 %reduce-scatter.2.cloned.1.call-done = f32[320,128]{1,0:T(8,128)} async-done(((f32[320,512]{1,0:T(8,128)}), f32[320,128]{1,0:T(8,128)}) %reduce-scatter.2.cloned.1.call-update) | async-done | bytes 163856 | tf_op jit(solution)/shard_map/reduce_scatter | solution.py:95
  101.9 1.1 convolution_convert_fusion.1
  103.6 5.5 %all-to-all-start = ((bf16[8,2,320]{2,1,0:T(2,128)(2,1)}), bf16[8,2,320]{2,1,0:T(2,128)(2,1)S(1)}, u32[]{:S(2)}, u32[]{:S(2)}) async-start(bf16[8,2,320]{2,1,0:T(2,128)(2,1)} %reshape.63), calls=%async_computation.1 | async-start | bytes 24576 | tf_op jit(solution)/shard_map/all_to_all | solution.py:109
  109.2 6.5 %all-to-all-done = bf16[8,2,320]{2,1,0:T(2,128)(2,1)S(1)} async-done(((bf16[8,2,320]{2,1,0:T(2,128)(2,1)}), bf16[8,2,320]{2,1,0:T(2,128)(2,1)S(1)}, u32[]{:S(2)}, u32[]{:S(2)}) %all-to-all-start) | async-done | bytes 10272 | tf_op jit(solution)/shard_map/all_to_all | solution.py:109
  115.8 7.7 %while.22 = (s32[]{:T(128)}, f32[8,2,128]{2,1,0:T(2,128)S(1)}, s32[8,2,128]{2,1,0:T(2,128)}, f32[8,2,640]{2,0,1:T(8,128)S(1)}) while((s32[]{:T(128)}, f32[8,2,128]{2,1,0:T(2,128)S(1)}, s32[8,2,128]{2,1,0:T(2,128)}, f32[8,2,640]{2,0,1:T(8,128)S(1)}) %tuple.68), condition=%wide.region_3.4_spmd.clone, body=%wide.region_1.3_spmd.sunk.clone | while | flops 491266 | bytes 31809 | solution.py:125
  115.9 0.7 dynamic-slice_bitcast_fusion.9
  116.8 0.7 dynamic-slice_bitcast_fusion.9
  117.8 0.7 dynamic-slice_bitcast_fusion.9
  118.7 0.7 dynamic-slice_bitcast_fusion.9
  119.7 0.7 dynamic-slice_bitcast_fusion.9
  120.7 0.7 dynamic-slice_bitcast_fusion.9
  121.6 0.7 dynamic-slice_bitcast_fusion.9
  122.6 0.7 dynamic-slice_bitcast_fusion.9
  124.2 7.1 %while.23 = (s32[]{:T(128)}, bf16[8,2,640]{2,1,0:T(2,128)(2,1)S(1)}, s32[8,2,128]{2,1,0:T(2,128)}, f32[8,2,128]{2,1,0:T(2,128)S(1)}) while((s32[]{:T(128)}, bf16[8,2,640]{2,1,0:T(2,128)(2,1)S(1)}, s32[8,2,128]{2,1,0:T(2,128)}, f32[8,2,128]{2,1,0:T(2,128)S(1)}) %tuple.69), condition=%wide.region_6.7_spmd.clone, body=%wide.region_4.6_spmd.sunk.clone | while | flops 490242 | bytes 13889 | solution.py:140
  125.1 0.7 dynamic-slice_bitcast_fusion.11
  126.0 0.7 dynamic-slice_bitcast_fusion.11
  126.9 0.7 dynamic-slice_bitcast_fusion.11
  128.7 0.7 dynamic-slice_bitcast_fusion.11
  130.5 0.7 dynamic-slice_bitcast_fusion.11
  131.6 8.9 %all_to_all.10 = bf16[8,2,320]{2,1,0:T(2,128)(2,1)S(1)} all-to-all(bf16[8,2,320]{2,1,0:T(2,128)(2,1)S(1)} %reshape.64), channel_id=1, replica_groups=mesh['tile'=8,'mem'=4] {'tile'}, dimensions={0} | all-to-all | bytes 20480 | tf_op jit(solution)/shard_map/all_to_all | solution.py:152
  140.8 6.0 %all_gather.3 = bf16[320,512]{1,0:T(8,128)(2,1)S(1)} all-gather(bf16[320,128]{1,0:T(8,128)(2,1)S(1)} %convolution_convert_fusion), channel_id=1, replica_groups=mesh['tile'=8,'mem'=4] {'mem'}, dimensions={1}, use_global_device_ids=true | all-gather | bytes 409600 | tf_op jit(solution)/shard_map/all_gather | solution.py:165
  146.8 3.9 %multiply_reduce_fusion = f32[64,512,16]{1,0,2:T(8,128)S(1)} fusion(f32[64,512,5]{1,0,2:T(8,128)S(1)} %convert.2, bf16[16,5,64,512]{3,2,1,0:T(8,128)(2,1)} %param.13), kind=kLoop, calls=%fused_computation.11 | loop fusion | flops 7340032 | bytes 7995392 | tf_op jit(solution)/shard_map/roug,oug->rug/dot_general | solution.py:170
  151.2 2.5 %collective-permute-start.2 = (f32[16,64,256]{2,1,0:T(8,128)S(1)}, f32[16,64,256]{2,1,0:T(8,128)S(1)}, u32[]{:S(2)}, u32[]{:S(2)}) collective-permute-start(f32[16,64,256]{2,1,0:T(8,128)S(1)} %get-tuple-element.96), channel_id=1, source_target_pairs={{0,4},{4,8},{8,12},{12,16},{16,20},{20,24},{24,28},{1,5},{5,9},{9,... | collective-permute-start | bytes 3145736 | tf_op jit(solution)/shard_map/ppermute | solution.py:19
  153.7 1.3 collective-permute-start.3
  155.0 44.0 %collective-permute-done.2 = f32[16,64,256]{2,1,0:T(8,128)S(1)} collective-permute-done((f32[16,64,256]{2,1,0:T(8,128)S(1)}, f32[16,64,256]{2,1,0:T(8,128)S(1)}, u32[]{:S(2)}, u32[]{:S(2)}) %collective-permute-start.2) | collective-permute-done | bytes 1048608 | tf_op jit(solution)/shard_map/ppermute | solution.py:19
  199.6 2.0 fusion.96
  201.6 2.5 %fusion.4 = f32[16,64,896]{2,1,0:T(8,128)S(1)} fusion(f32[16,64,1024]{2,1,0:T(8,128)S(1)} %pad_maximum_fusion, f32[16,64,895]{2,1,0:T(8,128)S(1)} %get-tuple-element.81, f32[16,64,895]{2,1,0:T(8,128)S(1)} %get-tuple-element.80, pred[896]{0:T(1024)(128)(4,1)S(1)} %copy-done.12, pred[896]{0:T(1024)(128)(4,1)S(1)} %copy-done.14, pred[896]{0:T(1024)(128)(4,1)S(1)} %copy-done.22), kind=kLoop, calls=%fused_computation.19 | loop fusion | flops 9175040 | bytes 22014592 | tf_op jit(solution)/shard_map/jit(_where)/select_n | solution.py:50
  204.1 1.7 fusion.98
  205.8 2.0 fusion.14
  207.8 1.4 fusion.100
  209.3 1.4 fusion.24
  210.7 1.1 fusion.102
  211.9 2.6 %fusion.34 = f32[16,64,512]{2,1,0:T(8,128)} fusion(f32[16,64,640]{2,1,0:T(8,128)S(1)} %fusion.24, f32[16,64,511]{2,1,0:T(8,128)S(1)} %get-tuple-element.93, f32[16,64,511]{2,1,0:T(8,128)S(1)} %get-tuple-element.92, pred[512]{0:T(512)(128)(4,1)S(1)} %copy-done.26, pred[512]{0:T(512)(128)(4,1)S(1)} %copy-done.28, pred[512]{0:T(512)(128)(4,1)S(1)} %copy-done.24), kind=kLoop, calls=%fused_computation.55 | loop fusion | flops 5242880 | bytes 12576256 | tf_op jit(solution)/shard_map/jit(_where)/select_n | solution.py:50
  (157 shorter events, 9.6 us)
Async XLA Ops:
  7.2 108.5 %copy-start = (bf16[640,320]{0,1:T(8,128)(2,1)S(1)}, bf16[640,320]{0,1:T(8,128)(2,1)}, u32[]{:S(2)}) copy-start(bf16[640,320]{0,1:T(8,128)(2,1)} %param.14) | copy-start | bytes 1228804
  7.2 54.7 %copy-start.2 = (f32[16,64,512]{2,1,0:T(8,128)S(1)}, f32[16,64,512]{2,1,0:T(8,128)}, u32[]{:S(2)}) copy-start(f32[16,64,512]{2,1,0:T(8,128)} %param.12) | copy-start | bytes 6291460
  7.2 94.7 %reduce-scatter.2.cloned.1.call-start = ((), (), s32[]{:S(2)}) async-start(), calls=%async_computation.3 | async-start | bytes 819200 | tf_op jit(solution)/shard_map/reduce_scatter | solution.py:95
  10.5 50.0 %collective-permute-start = (f32[16,64,256]{2,1,0:T(8,128)}, f32[16,64,256]{2,1,0:T(8,128)}, u32[]{:S(2)}, u32[]{:S(2)}) collective-permute-start(f32[16,64,256]{2,1,0:T(8,128)} %get-tuple-element.99), channel_id=1, source_target_pairs={{0,4},{4,8},{8,12},{12,16},{16,20},{20,24},{24,28},{1,5},{5,9},{9,... | collective-permute-start | bytes 3145736 | tf_op jit(solution)/shard_map/ppermute | solution.py:19
  16.3 45.8 %collective-permute-start.1 = (f32[16,64,256]{2,1,0:T(8,128)}, f32[16,64,256]{2,1,0:T(8,128)S(1)}, u32[]{:S(2)}, u32[]{:S(2)}) collective-permute-start(f32[16,64,256]{2,1,0:T(8,128)} %get-tuple-element.98), channel_id=1, source_target_pairs={{4,0},{8,4},{12,8},{16,12},{20,16},{24,20},{28,24},{5,1},{9,5},{13... | collective-permute-start | bytes 3145736 | tf_op jit(solution)/shard_map/ppermute | solution.py:22
  17.6 56.8 %copy-start.23 = (pred[512]{0:T(512)(128)(4,1)}, pred[512]{0:T(512)(128)(4,1)S(1)}, u32[]{:S(2)}) copy-start(pred[512]{0:T(512)(128)(4,1)S(1)} %get-tuple-element.108) | copy-start | bytes 1540
  17.6 56.8 %copy-start.25 = (pred[512]{0:T(512)(128)(4,1)}, pred[512]{0:T(512)(128)(4,1)S(1)}, u32[]{:S(2)}) copy-start(pred[512]{0:T(512)(128)(4,1)S(1)} %get-tuple-element.109) | copy-start | bytes 1540
  17.7 56.8 %copy-start.27 = (pred[512]{0:T(512)(128)(4,1)}, pred[512]{0:T(512)(128)(4,1)S(1)}, u32[]{:S(2)}) copy-start(pred[512]{0:T(512)(128)(4,1)S(1)} %broadcast_compare_fusion.1) | copy-start | bytes 1540
  17.7 46.5 %copy-start.21 = (pred[896]{0:T(1024)(128)(4,1)}, pred[896]{0:T(1024)(128)(4,1)S(1)}, u32[]{:S(2)}) copy-start(pred[896]{0:T(1024)(128)(4,1)S(1)} %fusion.88) | copy-start | bytes 2692
  17.7 50.7 %copy-start.19 = (pred[768]{0:T(1024)(128)(4,1)}, pred[768]{0:T(1024)(128)(4,1)S(1)}, u32[]{:S(2)}) copy-start(pred[768]{0:T(1024)(128)(4,1)S(1)} %fusion.89) | copy-start | bytes 2308
  17.7 54.1 %copy-start.17 = (pred[640]{0:T(1024)(128)(4,1)}, pred[640]{0:T(1024)(128)(4,1)S(1)}, u32[]{:S(2)}) copy-start(pred[640]{0:T(1024)(128)(4,1)S(1)} %fusion.90) | copy-start | bytes 1924
  17.8 46.5 %copy-start.11 = (pred[896]{0:T(1024)(128)(4,1)}, pred[896]{0:T(1024)(128)(4,1)S(1)}, u32[]{:S(2)}) copy-start(pred[896]{0:T(1024)(128)(4,1)S(1)} %get-tuple-element.102) | copy-start | bytes 2692
  17.8 46.5 %copy-start.13 = (pred[896]{0:T(1024)(128)(4,1)}, pred[896]{0:T(1024)(128)(4,1)S(1)}, u32[]{:S(2)}) copy-start(pred[896]{0:T(1024)(128)(4,1)S(1)} %get-tuple-element.103) | copy-start | bytes 2692
  17.8 50.6 %copy-start.7 = (pred[768]{0:T(1024)(128)(4,1)}, pred[768]{0:T(1024)(128)(4,1)S(1)}, u32[]{:S(2)}) copy-start(pred[768]{0:T(1024)(128)(4,1)S(1)} %get-tuple-element.104) | copy-start | bytes 2308
  17.8 50.6 %copy-start.9 = (pred[768]{0:T(1024)(128)(4,1)}, pred[768]{0:T(1024)(128)(4,1)S(1)}, u32[]{:S(2)}) copy-start(pred[768]{0:T(1024)(128)(4,1)S(1)} %get-tuple-element.105) | copy-start | bytes 2308
  17.8 54.0 %copy-start.3 = (pred[640]{0:T(1024)(128)(4,1)}, pred[640]{0:T(1024)(128)(4,1)S(1)}, u32[]{:S(2)}) copy-start(pred[640]{0:T(1024)(128)(4,1)S(1)} %get-tuple-element.106) | copy-start | bytes 1924
  17.8 54.0 %copy-start.5 = (pred[640]{0:T(1024)(128)(4,1)}, pred[640]{0:T(1024)(128)(4,1)S(1)}, u32[]{:S(2)}) copy-start(pred[640]{0:T(1024)(128)(4,1)S(1)} %get-tuple-element.107) | copy-start | bytes 1924
  73.3 2.4 %slice-start = ((s8[5242880]{0:T(1024)(128)(4,1)}), s8[4194304]{0:T(1024)(128)(4,1)S(1)}, s32[]{:S(2)}) async-start(s8[5242880]{0:T(1024)(128)(4,1)} %bitcast.65), calls=%async_computation.4 | async-start | bytes 8388608
  74.5 1.5 slice-start.1
  76.0 2.0 copy-start.29
  76.0 33.1 %copy-start.30 = (s32[1,8]{1,0:T(1,128)S(1)}, s32[1,8]{1,0:T(1,128)}, u32[]{:S(2)}) copy-start(s32[1,8]{1,0:T(1,128)} %param.16) | copy-start | bytes 100
  76.0 47.5 %copy-start.15 = (f32[1,8,2,128]{3,2,1,0:T(2,128)S(1)}, f32[1,8,2,128]{3,2,1,0:T(2,128)}, u32[]{:S(2)}) copy-start(f32[1,8,2,128]{3,2,1,0:T(2,128)} %param.18) | copy-start | bytes 24580
  76.0 47.5 %copy-start.16 = (f32[1,8,2,128]{3,2,1,0:T(2,128)S(1)}, f32[1,8,2,128]{3,2,1,0:T(2,128)}, u32[]{:S(2)}) copy-start(f32[1,8,2,128]{3,2,1,0:T(2,128)} %param.19) | copy-start | bytes 24580
  103.6 12.1 %all-to-all-start = ((bf16[8,2,320]{2,1,0:T(2,128)(2,1)}), bf16[8,2,320]{2,1,0:T(2,128)(2,1)S(1)}, u32[]{:S(2)}, u32[]{:S(2)}) async-start(bf16[8,2,320]{2,1,0:T(2,128)(2,1)} %reshape.63), calls=%async_computation.1 | async-start | bytes 24576 | tf_op jit(solution)/shard_map/all_to_all | solution.py:109
  151.2 47.8 %collective-permute-start.2 = (f32[16,64,256]{2,1,0:T(8,128)S(1)}, f32[16,64,256]{2,1,0:T(8,128)S(1)}, u32[]{:S(2)}, u32[]{:S(2)}) collective-permute-start(f32[16,64,256]{2,1,0:T(8,128)S(1)} %get-tuple-element.96), channel_id=1, source_target_pairs={{0,4},{4,8},{8,12},{12,16},{16,20},{20,24},{24,28},{1,5},{5,9},{9,... | collective-permute-start | bytes 3145736 | tf_op jit(solution)/shard_map/ppermute | solution.py:19
  153.7 45.3 %collective-permute-start.3 = (f32[16,64,256]{2,1,0:T(8,128)S(1)}, f32[16,64,256]{2,1,0:T(8,128)S(1)}, u32[]{:S(2)}, u32[]{:S(2)}) collective-permute-start(f32[16,64,256]{2,1,0:T(8,128)S(1)} %get-tuple-element.97), channel_id=1, source_target_pairs={{4,0},{8,4},{12,8},{16,12},{20,16},{24,20},{28,24},{5,1},{9,5},{13... | collective-permute-start | bytes 3145736 | tf_op jit(solution)/shard_map/ppermute | solution.py:22
  199.6 2.0 copy-start.12
  199.6 2.0 copy-start.14
  199.6 2.0 copy-start.22
  204.1 1.7 copy-start.8
  204.1 1.7 copy-start.10
  204.1 1.7 copy-start.20
  207.8 1.4 copy-start.4
  207.8 1.4 copy-start.6
  207.8 1.4 copy-start.18
  210.7 1.2 copy-start.24
  210.7 1.2 copy-start.26
  210.7 1.2 copy-start.28
  211.9 2.6 %copy-start.1 = (bf16[640,320]{0,1:T(8,128)(2,1)S(1)}, bf16[640,320]{0,1:T(8,128)(2,1)}, u32[]{:S(2)}) copy-start(bf16[640,320]{0,1:T(8,128)(2,1)} %param.14) | copy-start | bytes 1228804
Sparse Core Ops, SparseCore 0:
  78.2 23.6 reduce-scatter.1
where the time goes:
time: 223 us; the launch traced here: 221 us
  waiting for transfers between devices  117 us (52%)
  local copies, waits for them, and re-layouts  30.4 us (14%)
  other arithmetic  26 us (12%)
  starting transfers between devices  16.4 us (7%)
  blocking collectives  14.9 us (7%)
  between operations  14.7 us (7%)
    ppermute x2, waiting for transfers between devices, extended_2(): lax.ppermute(lax.slice_in_dim(block, block.shape[dim] - width, None, axis...  86.7 us
    reduce_scatter x1, waiting for transfers between devices, body(): lax.psum_scatter(member_sum, 'mem', scatter_dimension=1, tiled=True)  23.7 us
    select_n x7, other arithmetic, localize(): jnp.where((domain_wide_row >= 0) & (domain_wide_row < grid_rows), swept,...  14.3 us
    slice x8, local copies, waits for them, and re-layouts, y_neighbours(): upward = jnp.concatenate([state_field[..., 1:], zeros_edge], -1)  12.4 us
    all_to_all x1, blocking collectives, body(): lax.all_to_all(column_adjoint.reshape(owner_count, count_of_slots, state_...  8.91 us
    ppermute x2, starting transfers between devices, extended_2(): lax.ppermute(lax.slice_in_dim(block, block.shape[dim] - width, None, axis...  8.32 us
    all_to_all x1, waiting for transfers between devices, body(): lax.all_to_all(outgoing.reshape(owner_count, count_of_slots, state_size),...  6.47 us
    all_gather x1, blocking collectives, body(): strip_adjoint = lax.all_gather(block_adjoint, 'mem', axis=1, tiled=True)  5.99 us
  transfers between devices with their start and end apart: 6, of which 4 were waited for; matrix products, arithmetic and copies ran while one was open for 1% of the time, Pallas kernels for 0%

commit v1 on v0

v1 whole, which is shorter than its diff:
```python
import math

import jax
import jax.numpy as jnp
import numpy as np
from jax import lax
from jax.sharding import PartitionSpec as P

NY = 64
SWEEPS = 4
SWEEP_SCALE = 0.2**SWEEPS


def sweep_counts(strip_rows, low_wall, high_wall):
    rows = strip_rows + 2 * SWEEPS
    field = np.zeros((strip_rows * NY, rows, NY), np.float32)
    for row in range(strip_rows):
        for y in range(NY):
            field[row * NY + y, row + SWEEPS, y] = 1.0
    inside = np.ones((rows, 1), np.float32)
    if low_wall:
        inside[:SWEEPS] = 0.0
    if high_wall:
        inside[rows - SWEEPS :] = 0.0
    for _ in range(SWEEPS):
        padded = np.pad(field, ((0, 0), (1, 1), (1, 1)))
        field = field + padded[:, 2:, 1:-1] + padded[:, :-2, 1:-1]
        field = (field + padded[:, 1:-1, 2:] + padded[:, 1:-1, :-2]) * inside
    return field.reshape(strip_rows * NY, rows * NY)


def split_two(values):
    high = lax.reduce_precision(values, 8, 7)
    return high.astype(jnp.bfloat16), (values - high).astype(jnp.bfloat16)


def dot_two(values, table, contract):
    high, low = split_two(values)
    dims = (((values.ndim - 1,), (contract,)), ((), ()))
    return SWEEP_SCALE * (
        lax.dot_general(high, table, dims, preferred_element_type=jnp.float32)
        + lax.dot_general(low, table, dims, preferred_element_type=jnp.float32)
    )


def body(
    control,
    ensemble,
    jacobian,
    send_columns,
    received_counts,
    observed_channel,
    innovation,
    error_weight,
):
    tiles = lax.axis_size("tile")
    groups = lax.axis_size("mem")
    tile_index = lax.axis_index("tile")
    members_here, levels, strip = control.shape
    variables = ensemble.shape[1]
    state = variables * levels
    member_scale = 1.0 / math.sqrt(members_here * groups)
    block = strip // groups
    owners, cap = send_columns.shape[1:]
    slots = owners * cap
    halo = SWEEPS * NY
    edge_blocks = -(-halo // block)
    edge = edge_blocks * slots
    own = groups * slots

    tables = lax.all_gather(send_columns[0].reshape(slots), ("tile", "mem"))
    tables = tables.reshape(tiles, groups, slots)
    tables = tables + (lax.iota(jnp.int32, groups) * block)[None, :, None]
    padded = jnp.pad(tables, ((1, 1), (0, 0), (0, 0)), constant_values=-4 * strip)
    near = lax.dynamic_slice_in_dim(padded, tile_index, 3, 0)
    left = near[0, groups - edge_blocks :].reshape(edge) - strip
    right = near[2, :edge_blocks].reshape(edge) + strip
    middle = near[1].reshape(own)
    carried = jnp.concatenate([left, middle, right])
    width = strip + 2 * halo
    hits = (lax.iota(jnp.int32, width)[:, None] == carried[None, :] + halo).astype(jnp.bfloat16)
    kinds = np.stack([
        sweep_counts(strip // NY, low, high) for low in (False, True) for high in (False, True)
    ]).astype(jnp.bfloat16)
    kind = 2 * (tile_index == 0).astype(jnp.int32) + (tile_index == tiles - 1).astype(jnp.int32)
    counts = lax.dynamic_index_in_dim(jnp.asarray(kinds), kind, 0, keepdims=False)
    spread = jnp.dot(counts, hits, preferred_element_type=jnp.float32).astype(jnp.bfloat16)

    partial = dot_two(control, spread, 0)
    forward = [(i, i + 1) for i in range(tiles - 1)]
    backward = [(i + 1, i) for i in range(tiles - 1)]
    from_right = lax.ppermute(partial[..., :edge], "tile", backward)
    from_left = lax.ppermute(partial[..., edge + own :], "tile", forward)
    localized = (
        partial[..., edge : edge + own]
        + jnp.pad(from_left, ((0, 0), (0, 0), (0, own - edge)))
        + jnp.pad(from_right, ((0, 0), (0, 0), (own - edge, 0)))
    )
    weights = localized.astype(jnp.bfloat16)
    own_hits = hits[halo : halo + strip, edge : edge + own]
    picked = lax.dot_general(
        ensemble, own_hits, (((3,), (0,)), ((), ())), preferred_element_type=jnp.float32
    )
    sums = jnp.sum(weights.astype(jnp.float32)[:, None] * picked, axis=0) * member_scale
    sums = jnp.transpose(sums.reshape(state, groups, owners, cap), (2, 1, 3, 0))
    parts = lax.all_to_all(
        sums.reshape(owners * groups, cap, state), ("tile", "mem"), 0, 0, tiled=True
    )
    incoming = jnp.sum(parts.reshape(owners, groups, cap, state), axis=1).astype(jnp.bfloat16)

    model = jnp.dot(
        incoming.reshape(slots, state), jnp.transpose(jacobian), preferred_element_type=jnp.float32
    )
    channels = jacobian.shape[0]
    observed = observed_channel.shape[-1]
    channel_rows = observed_channel[0].reshape(slots, observed)
    found = channel_rows[:, :, None] == lax.iota(jnp.int32, channels)[None, None, :]
    evolved = jnp.sum(jnp.where(found, model[:, None, :], 0.0), axis=2)
    evolved = evolved.reshape(owners, cap, observed)
    filled = (
        jnp.arange(cap, dtype=jnp.int32)[None, :, None] < received_counts[0][:, None, None]
    )
    departures = jnp.where(filled, evolved - innovation[0], 0.0)
    weighted = (error_weight[0] * departures).reshape(slots, observed)
    channel_adjoint = jnp.sum(jnp.where(found, weighted[:, :, None], 0.0), axis=1)
    column_adjoint = jnp.dot(
        channel_adjoint.astype(jnp.bfloat16), jacobian, preferred_element_type=jnp.float32
    ).astype(jnp.bfloat16)

    copies = jnp.broadcast_to(
        column_adjoint.reshape(owners, 1, cap, state), (owners, groups, cap, state)
    )
    returned = lax.all_to_all(
        copies.reshape(owners * groups, cap, state), ("tile", "mem"), 0, 0, tiled=True
    )
    returned = jnp.transpose(returned.reshape(owners, groups, cap, state), (3, 1, 0, 2))
    returned = returned.reshape(variables, levels, own).astype(jnp.float32)
    member_adjoint = jnp.sum(picked * returned[None], axis=1) * member_scale
    low = lax.ppermute(member_adjoint[..., own - edge :], "tile", forward)
    high = lax.ppermute(member_adjoint[..., :edge], "tile", backward)
    extended = jnp.concatenate([low, member_adjoint, high], axis=-1)
    gradient = dot_two(extended, spread, 1)
    return (gradient, departures[None])


def solution(mesh):
    in_specs = (
        P("mem", None, "tile"),
        P("mem", None, None, "tile"),
        P(),
        P(("tile", "mem"), None, None),
        P(("tile", "mem"), None),
        P(("tile", "mem"), None, None, None),
        P(("tile", "mem"), None, None, None),
        P(("tile", "mem"), None, None, None),
    )
    out_specs = (P("mem", None, "tile"), P(("tile", "mem"), None, None, None))
    return jax.shard_map(body, mesh=mesh, in_specs=in_specs, out_specs=out_specs, check_vma=False)
```

time: 223 us -> 135 us (0.61)
  waiting for transfers between devices: 117 us -> 48.1 us
  blocking collectives: 14.9 us -> 52 us
  local copies, waits for them, and re-layouts: 30.4 us -> 4.42 us
  other arithmetic: 26 us -> 7.24 us
  between operations: 14.7 us -> 0.95 us
  matrix products: 1.63 us -> 12.1 us
  starting transfers between devices: 16.4 us -> 9.28 us
    ppermute x4, waiting for transfers between devices: 86.7 us -> 41.6 us  [the longest x1 21 us: body(): from_left = lax.ppermute(partial[..., edge + own:], 'tile', forward)]
    all_gather x1, blocking collectives: 5.99 us -> 43 us  [body(): tables = lax.all_gather(send_columns[0].reshape(slots), ('tile', 'mem'))]
    reduce_scatter x1 -> x0, waiting for transfers between devices: 23.7 us -> none  [body(): lax.psum_scatter(member_sum, 'mem', scatter_dimension=1, tiled=True)]
    slice x10 -> x3, local copies, waits for them, and re-layouts: 15.9 us -> 0.43 us  [the longest x1 0.21 us: body(): from_left = lax.ppermute(partial[..., edge + own:], 'tile', forward)]
    select_n x7 -> x1, other arithmetic: 14.3 us -> 0.68 us  [body(): departures = jnp.where(filled, evolved - innovation[0], 0.0)]
    eq x17 -> x0, local copies, waits for them, and re-layouts: 11 us -> none  [the longest x8 5.49 us: pick_channels(): hits = channel_block[:, :, None] == channel_ids[None, None, :]]
    dot_general x3 -> x7, matrix products: 1.45 us -> 11.9 us  [the longest x1 5.17 us: body(): lax.dot_general(ensemble, own_hits, (((3,), (0,)), ((), ())), preferred_e...]
    dot_general x2 -> x0, other arithmetic: 5 us -> none  [the longest x1 3.91 us: body(): jnp.einsum('roug,oug->rug', ensemble, analysis_increment_adjoint, preferr...]
  transfers between devices with their start and end apart: 6 -> 5, of which waited for: 4 -> 3; matrix products, arithmetic and copies ran while one was open for 1% -> 2% of each run, Pallas kernels for 0% -> 0%
where the time goes in v1:
time: 135 us; the launch traced here: 134 us
  blocking collectives  52 us (39%)
  waiting for transfers between devices  48.1 us (36%)
  matrix products  12.1 us (9%)
  starting transfers between devices  9.28 us (7%)
  other arithmetic  7.24 us (5%)
  local copies, waits for them, and re-layouts  4.42 us (3%)
    all_gather x1, blocking collectives, body(): tables = lax.all_gather(send_columns[0].reshape(slots), ('tile', 'mem'))  43 us
    ppermute x1, waiting for transfers between devices, body(): from_left = lax.ppermute(partial[..., edge + own:], 'tile', forward)  21 us
    ppermute x1, waiting for transfers between devices, body(): low = lax.ppermute(member_adjoint[..., own - edge:], 'tile', forward)  20.6 us
    all_to_all x1, blocking collectives, body(): lax.all_to_all(copies.reshape(owners * groups, cap, state), ('tile', 'mem...  9.03 us
    all_to_all x1, waiting for transfers between devices, body(): lax.all_to_all(sums.reshape(owners * groups, cap, state), ('tile', 'mem')...  6.54 us
    dot_general x1, matrix products, body(): lax.dot_general(ensemble, own_hits, (((3,), (0,)), ((), ())), preferred_e...  5.17 us
    dot_general x2, matrix products, dot_two(): lax.dot_general(high, table, dims, preferred_element_type=jnp.float32)  3.89 us
    all_to_all x1, starting transfers between devices, body(): lax.all_to_all(sums.reshape(owners * groups, cap, state), ('tile', 'mem')...  2.85 us
  transfers between devices with their start and end apart: 5, of which 3 were waited for; matrix products, arithmetic and copies ran while one was open for 2% of the time, Pallas kernels for 0%

profile of v1, /device:TPU:0, one launch (start us, length us, event | category | flops | bytes accessed | tf_op | source)
XLA Modules:
  0.0 134.2 jit_solution(17920015109685909607)
XLA Ops:
  0.6 0.0 copy-start
  0.6 0.0 copy-start.1
  0.7 0.9 copy.29
  1.6 0.1 reshape.136
  1.7 43.0 %all-gather = s32[32,1,16]{2,1,0:T(1,128)S(1)} all-gather(s32[1,1,16]{2,1,0:T(1,128)S(1)} %reshape.136), channel_id=1, replica_groups=mesh['tile'=8,'mem'=4] {'tile','mem'}, dimensions={0}, use_global_device_ids=true | all-gather | bytes 2112 | tf_op jit(solution)/shard_map/all_gather | solution.py:71
  44.7 0.1 broadcast_add_fusion
  44.8 0.1 concatenate.12
  44.9 0.1 sub.22
  45.0 0.1 add.63
  45.0 0.1 add_add_fusion
  45.1 1.8 %fusion.4 = bf16[512,128,1]{1,0,2:T(8,128)(2,1)S(1)} fusion(bf16[4,512,1024]{2,1,0:T(8,128)(2,1)} %constant.41.clone, s32[]{:T(128)S(6)} %select_n.27, s32[128]{0:T(128)S(1)} %add_add_fusion), kind=kOutput, calls=%fused_computation.15 | convolution fusion | flops 134414336 | bytes 1180164 | tf_op jit(solution)/shard_map/dot_general | solution.py:87
  46.9 2.1 %convolution_bitcast_fusion = f32[16,64,128]{2,1,0:T(8,128)S(1)} fusion(bf16[512,128,1]{1,0,2:T(8,128)(2,1)S(1)} %fusion.4, f32[16,64,512]{2,1,0:T(8,128)} %param.9), kind=kOutput, calls=%fused_computation.13 | convolution fusion | flops 135266304 | bytes 2752512 | tf_op jit(solution)/shard_map/dot_general | solution.py:41
  49.0 0.4 fusion.3
  49.4 0.2 fusion.20
  49.6 1.3 collective-permute-start
  51.0 1.3 collective-permute-start.1
  52.3 0.8 iota_compare_fusion.1
  53.1 21.0 %collective-permute-done = f32[16,64,32]{2,1,0:T(8,128)S(1)} collective-permute-done((f32[16,64,32]{2,1,0:T(8,128)S(1)}, f32[16,64,32]{2,1,0:T(8,128)S(1)}, u32[]{:S(2)}, u32[]{:S(2)}) %collective-permute-start) | collective-permute-done | bytes 131104 | tf_op jit(solution)/shard_map/ppermute | solution.py:93
  74.1 0.3 fusion.11
  74.4 0.2 copy.30
  74.6 5.2 %fusion = (f32[5,64,64]{1,2,0:T(8,128)S(1)}, f32[64,16,5,64]{3,0,2,1:T(8,128)S(1)}) fusion(f32[16,64,64]{1,2,0:T(8,128)S(1)} %copy.30, bf16[16,5,64,512]{3,2,1,0:T(8,128)(2,1)} %param.10, pred[1024,128]{0,1:T(32,128)(4,1)} %iota_compare_fusion.1), kind=kOutput, calls=%fused_computation.7 | convolution fusion | flops 336179200 | bytes 6930432 | tf_op jit(solution)/shard_map/dot_general | solution.py:101
  79.8 0.1 copy.31
  79.9 0.1 mul.65
  80.1 0.7 copy.32
  80.7 2.8 %all-to-all-start = ((f32[32,2,320]{2,1,0:T(2,128)}), f32[32,2,320]{2,1,0:T(2,128)S(1)}, u32[]{:S(2)}, u32[]{:S(2)}) async-start(f32[32,2,320]{2,1,0:T(2,128)} %bitcast.11), calls=%async_computation | async-start | bytes 196608 | tf_op jit(solution)/shard_map/all_to_all | solution.py:106
  83.6 0.7 iota_compare_fusion.3
  84.3 0.1 lt.36
  84.4 0.5 copy-done.7
  84.8 6.5 %all-to-all-done = f32[32,2,320]{2,1,0:T(2,128)S(1)} async-done(((f32[32,2,320]{2,1,0:T(2,128)}), f32[32,2,320]{2,1,0:T(2,128)S(1)}, u32[]{:S(2)}, u32[]{:S(2)}) %all-to-all-start) | async-done | bytes 81952 | tf_op jit(solution)/shard_map/all_to_all | solution.py:106
  91.5 0.2 fusion.21
  91.6 1.7 %select_reduce_fusion.1 = f32[16,128]{1,0:T(8,128)S(1)} fusion(f32[16,640]{1,0:T(8,128)S(1)} %fusion.21, s32[16,128]{1,0:T(8,128)} %bitcast.54), kind=kLoop, calls=%fused_computation.1 | loop fusion | flops 3930112 | bytes 57344 | tf_op jit(solution)/shard_map/reduce_sum | solution.py:118
  93.3 0.6 copy-done.4
  93.9 0.8 select_multiply_fusion
  94.7 1.6 %select_reduce_fusion = bf16[16,640]{1,0:T(8,128)(2,1)S(1)} fusion(f32[16,128]{1,0:T(8,128)S(1)} %select_multiply_fusion, s32[16,128]{1,0:T(8,128)} %bitcast.55), kind=kLoop, calls=%fused_computation | loop fusion | flops 3921920 | bytes 36864 | tf_op jit(solution)/shard_map/reduce_sum | solution.py:125
  96.3 0.2 convolution_convert_fusion.1
  96.5 0.1 broadcast_in_dim.59
  96.6 9.0 %all_to_all.10 = bf16[32,2,320]{2,1,0:T(2,128)(2,1)S(1)} all-to-all(bf16[32,2,320]{2,1,0:T(2,128)(2,1)S(1)} %bitcast.50), channel_id=1, replica_groups=mesh['tile'=8,'mem'=4] {'tile','mem'}, dimensions={0} | all-to-all | bytes 81920 | tf_op jit(solution)/shard_map/all_to_all | solution.py:133
  105.7 0.1 reshape.134
  105.9 0.3 fusion.1
  106.2 0.0 copy-start.6
  106.3 0.2 copy.35
  106.5 0.2 fusion.19
  106.7 2.5 %collective-permute-start.2 = (f32[16,64,32]{2,1,0:T(8,128)S(1)}, f32[16,64,32]{2,1,0:T(8,128)S(1)}, u32[]{:S(2)}, u32[]{:S(2)}) collective-permute-start(f32[16,64,32]{2,1,0:T(8,128)S(1)} %get-tuple-element.2), channel_id=1, source_target_pairs={{0,4},{4,8},{8,12},{12,16},{16,20},{20,24},{24,28},{1,5},{5,9},{9,... | collective-permute-start | bytes 393224 | tf_op jit(solution)/shard_map/ppermute | solution.py:139
  109.3 1.3 collective-permute-start.3
  110.6 0.7 subtract_select_fusion
  111.3 20.6 %collective-permute-done.2 = f32[16,64,32]{2,1,0:T(8,128)S(1)} collective-permute-done((f32[16,64,32]{2,1,0:T(8,128)S(1)}, f32[16,64,32]{2,1,0:T(8,128)S(1)}, u32[]{:S(2)}, u32[]{:S(2)}) %collective-permute-start.2) | collective-permute-done | bytes 131104 | tf_op jit(solution)/shard_map/ppermute | solution.py:139
  131.9 0.5 fusion.12
  132.4 1.8 %add_multiply_fusion = f32[16,64,512]{2,1,0:T(8,128)} fusion(f32[16,64,512]{2,1,0:T(8,128)S(1)} %fusion.12, bf16[512,128,1]{1,0,2:T(8,128)(2,1)S(1)} %copy-done.3, f32[16,64,32]{2,1,0:T(8,128)S(1)} %collective-permute-done.3, f32[16,64,64]{2,1,0:T(8,128)S(1)} %broadcast_multiply_fusion, f32[16,64,32]{2,1,0:T(8,128)S(1)} %collective-permute-done.2), kind=kOutput, calls=%fused_computation.10 | convolution fusion | flops 135790592 | bytes 4849664 | tf_op jit(solution)/shard_map/dot_general | solution.py:41
  (26 shorter events, 0.3 us)
Async XLA Ops:
  0.6 90.8 %copy-start = (bf16[640,320]{0,1:T(8,128)(2,1)S(1)}, bf16[640,320]{0,1:T(8,128)(2,1)}, u32[]{:S(2)}) copy-start(bf16[640,320]{0,1:T(8,128)(2,1)} %param.11) | copy-start | bytes 1228804
  0.6 48.3 %copy-start.1 = (f32[16,64,512]{2,1,0:T(8,128)S(1)}, f32[16,64,512]{2,1,0:T(8,128)}, u32[]{:S(2)}) copy-start(f32[16,64,512]{2,1,0:T(8,128)} %param.9) | copy-start | bytes 6291460
  46.9 2.6 %copy-start.2 = (bf16[512,128,1]{1,0,2:T(8,128)(2,1)}, bf16[512,128,1]{1,0,2:T(8,128)(2,1)S(1)}, u32[]{:S(2)}) copy-start(bf16[512,128,1]{1,0,2:T(8,128)(2,1)S(1)} %fusion.4) | copy-start | bytes 393220
  49.6 24.4 %collective-permute-start = (f32[16,64,32]{2,1,0:T(8,128)S(1)}, f32[16,64,32]{2,1,0:T(8,128)S(1)}, u32[]{:S(2)}, u32[]{:S(2)}) collective-permute-start(f32[16,64,32]{2,1,0:T(8,128)S(1)} %get-tuple-element.4), channel_id=1, source_target_pairs={{0,4},{4,8},{8,12},{12,16},{16,20},{20,24},{24,28},{1,5},{5,9},{9,... | collective-permute-start | bytes 393224 | tf_op jit(solution)/shard_map/ppermute | solution.py:93
  51.0 23.1 %collective-permute-start.1 = (f32[16,64,32]{2,1,0:T(8,128)S(1)}, f32[16,64,32]{2,1,0:T(8,128)S(1)}, u32[]{:S(2)}, u32[]{:S(2)}) collective-permute-start(f32[16,64,32]{2,1,0:T(8,128)S(1)} %get-tuple-element.5), channel_id=1, source_target_pairs={{4,0},{8,4},{12,8},{16,12},{20,16},{24,20},{28,24},{5,1},{9,5},{13... | collective-permute-start | bytes 393224 | tf_op jit(solution)/shard_map/ppermute | solution.py:92
  80.7 10.7 %all-to-all-start = ((f32[32,2,320]{2,1,0:T(2,128)}), f32[32,2,320]{2,1,0:T(2,128)S(1)}, u32[]{:S(2)}, u32[]{:S(2)}) async-start(f32[32,2,320]{2,1,0:T(2,128)} %bitcast.11), calls=%async_computation | async-start | bytes 196608 | tf_op jit(solution)/shard_map/all_to_all | solution.py:106
  84.3 0.5 copy-start.7
  93.3 0.6 copy-start.4
  106.2 4.4 %copy-start.5 = (f32[16,128]{1,0:T(8,128)S(1)}, f32[16,128]{1,0:T(8,128)}, u32[]{:S(2)}) copy-start(f32[16,128]{1,0:T(8,128)} %copy-done.4) | copy-start | bytes 24580
  106.2 4.4 %copy-start.6 = (f32[1,8,2,128]{3,2,1,0:T(2,128)S(1)}, f32[1,8,2,128]{3,2,1,0:T(2,128)}, u32[]{:S(2)}) copy-start(f32[1,8,2,128]{3,2,1,0:T(2,128)} %param.15) | copy-start | bytes 24580
  106.2 4.3 %copy-start.8 = (pred[8,2]{1,0:T(8,128)(4,1)S(1)}, pred[8,2]{1,0:T(8,128)(4,1)}, u32[]{:S(2)}) copy-start(pred[8,2]{1,0:T(8,128)(4,1)} %copy-done.7) | copy-start | bytes 52
  106.2 25.6 %copy-start.3 = (bf16[512,128,1]{1,0,2:T(8,128)(2,1)S(1)}, bf16[512,128,1]{1,0,2:T(8,128)(2,1)}, u32[]{:S(2)}) copy-start(bf16[512,128,1]{1,0,2:T(8,128)(2,1)} %copy-done.2) | copy-start | bytes 393220
  106.7 25.1 %collective-permute-start.2 = (f32[16,64,32]{2,1,0:T(8,128)S(1)}, f32[16,64,32]{2,1,0:T(8,128)S(1)}, u32[]{:S(2)}, u32[]{:S(2)}) collective-permute-start(f32[16,64,32]{2,1,0:T(8,128)S(1)} %get-tuple-element.2), channel_id=1, source_target_pairs={{0,4},{4,8},{8,12},{12,16},{16,20},{20,24},{24,28},{1,5},{5,9},{9,... | collective-permute-start | bytes 393224 | tf_op jit(solution)/shard_map/ppermute | solution.py:139
  109.3 22.6 %collective-permute-start.3 = (f32[16,64,32]{2,1,0:T(8,128)S(1)}, f32[16,64,32]{2,1,0:T(8,128)S(1)}, u32[]{:S(2)}, u32[]{:S(2)}) collective-permute-start(f32[16,64,32]{2,1,0:T(8,128)S(1)} %get-tuple-element.3), channel_id=1, source_target_pairs={{4,0},{8,4},{12,8},{16,12},{20,16},{24,20},{28,24},{5,1},{9,5},{13... | collective-permute-start | bytes 393224 | tf_op jit(solution)/shard_map/ppermute | solution.py:140

commit v2 on v1

v2 whole, which is shorter than its diff:
```python
import math

import jax
import jax.numpy as jnp
import numpy as np
from jax import lax
from jax.experimental import pallas as pl
from jax.experimental.pallas import tpu as pltpu
from jax.sharding import PartitionSpec as P

NY = 64
SWEEPS = 4
SWEEP_SCALE = 0.2**SWEEPS


def sweep_counts(strip_rows, low_wall, high_wall):
    rows = strip_rows + 2 * SWEEPS
    field = np.zeros((strip_rows * NY, rows, NY), np.float32)
    for row in range(strip_rows):
        for y in range(NY):
            field[row * NY + y, row + SWEEPS, y] = 1.0
    inside = np.ones((rows, 1), np.float32)
    if low_wall:
        inside[:SWEEPS] = 0.0
    if high_wall:
        inside[rows - SWEEPS :] = 0.0
    for _ in range(SWEEPS):
        padded = np.pad(field, ((0, 0), (1, 1), (1, 1)))
        field = field + padded[:, 2:, 1:-1] + padded[:, :-2, 1:-1]
        field = (field + padded[:, 1:-1, 2:] + padded[:, 1:-1, :-2]) * inside
    return field.reshape(strip_rows * NY, rows * NY)


def split_two(values):
    high = lax.reduce_precision(values, 8, 7)
    return high.astype(jnp.bfloat16), (values - high).astype(jnp.bfloat16)


def split_in_kernel(values, terms):
    pieces = []
    for _ in range(terms):
        piece = values.astype(jnp.bfloat16)
        pieces.append(piece)
        values = values - piece.astype(jnp.float32)
    return pieces


def dot(left, right, dims):
    return lax.dot_general(left, right, (dims, ((), ())), preferred_element_type=jnp.float32)


NN = ((1,), (0,))
NT = ((1,), (1,))


def kernel(
    sizes,
    table_ref,
    counts_ref,
    fold_ref,
    jacobian_ref,
    filled_ref,
    channel_ref,
    innovation_ref,
    error_ref,
    control_hbm,
    ensemble_hbm,
    extended_ref,
    spread_ref,
    departures_ref,
    control_ref,
    ensemble_ref,
    tabs,
    partial,
    halo_in,
    picked,
    sums,
    sums_in,
    rows_out,
    rows_in,
    back_out,
    back_in,
    incoming,
    channel_adjoint,
    adjoint,
    local_sem,
    table_send,
    table_recv,
    near_send,
    near_recv,
    halo_send,
    halo_recv,
    sum_send,
    sum_recv,
    there_send,
    there_recv,
    back_send,
    back_recv,
    all_send,
    all_recv,
    last_send,
    last_recv,
):
    (tiles, groups, strip, block, owners, cap, edge, members_here, levels, variables, scale) = sizes
    slots = owners * cap
    own = groups * slots
    halo = SWEEPS * NY
    state = variables * levels
    pair = 128 // levels
    pairs = members_here // pair
    tile = lax.axis_index("tile")
    mem = lax.axis_index("mem")

    control_copy = pltpu.make_async_copy(control_hbm, control_ref, local_sem.at[0])
    ensemble_copy = pltpu.make_async_copy(ensemble_hbm, ensemble_ref, local_sem.at[1])
    control_copy.start()
    ensemble_copy.start()

    def to_mem(offset):
        return {"tile": tile, "mem": lax.rem(mem + offset, groups)}

    def to_tile(offset):
        return {"tile": lax.rem(tile + offset, tiles), "mem": mem}

    def send(source, target, send_sem, recv_sem, device):
        return pltpu.make_async_remote_copy(
            src_ref=source,
            dst_ref=target,
            send_sem=send_sem,
            recv_sem=recv_sem,
            device_id=device,
            device_id_type=pl.DeviceIdType.MESH,
        )

    barrier = pltpu.get_barrier_semaphore()
    for offset in range(1, groups):
        pl.semaphore_signal(
            barrier, inc=1, device_id=to_mem(offset), device_id_type=pl.DeviceIdType.MESH
        )
    for offset in range(1, tiles):
        pl.semaphore_signal(
            barrier, inc=1, device_id=to_tile(offset), device_id_type=pl.DeviceIdType.MESH
        )
    pl.semaphore_wait(barrier, groups + tiles - 2)

    def beside(low_source, high_source, low_target, high_target, send_sem, recv_sem):
        def downward():
            device = {"tile": tile - 1, "mem": mem}
            return send(low_source, high_target, send_sem.at[0], recv_sem.at[1], device)

        def upward():
            device = {"tile": tile + 1, "mem": mem}
            return send(high_source, low_target, send_sem.at[1], recv_sem.at[0], device)

        def start():
            @pl.when(tile > 0)
            def _():
                downward().start()

            @pl.when(tile < tiles - 1)
            def _():
                upward().start()

        def wait():
            @pl.when(tile > 0)
            def _():
                downward().wait_send()
                upward().wait_recv()

            @pl.when(tile < tiles - 1)
            def _():
                upward().wait_send()
                downward().wait_recv()

        return start, wait

    def over_mem(source_of, target, send_sem, recv_sem):
        copies = [
            send(source_of(offset), target, send_sem.at[offset - 1], recv_sem.at[offset - 1],
                 to_mem(offset))
            for offset in range(1, groups)
        ]
        for copy in copies:
            copy.start()
        return copies

    def over_tile(source, target, send_sem, recv_sem):
        copies = [
            send(source.at[lax.rem(tile + offset, tiles)], target.at[tile],
                 send_sem.at[offset - 1], recv_sem.at[offset - 1], to_tile(offset))
            for offset in range(1, tiles)
        ]
        for copy in copies:
            copy.start()
        return copies

    my_rows = tabs.at[pl.ds(pl.multiple_of(edge + mem * slots, 8), slots)]
    my_rows[...] = table_ref[...]

    @pl.when(tile == 0)
    def _():
        tabs[0:edge] = jnp.full((edge, 128), -8 * strip, jnp.int32)
        halo_in[0] = jnp.zeros_like(halo_in[0])
        extended_ref[0:edge] = jnp.zeros((edge, members_here * levels), jnp.float32)

    @pl.when(tile == tiles - 1)
    def _():
        tabs[edge + own :] = jnp.full((edge, 128), 8 * strip, jnp.int32)
        halo_in[1] = jnp.zeros_like(halo_in[1])
        extended_ref[edge + own :] = jnp.zeros((edge, members_here * levels), jnp.float32)

    for copy in over_mem(lambda offset: my_rows, my_rows, table_send, table_recv):
        copy.wait()
    start, wait = beside(
        tabs.at[edge : 2 * edge], tabs.at[own : own + edge],
        tabs.at[0:edge], tabs.at[edge + own :], near_send, near_recv,
    )
    start()
    wait()

    shift = jnp.concatenate([
        jnp.full((edge, 128), halo - strip, jnp.int32),
        jnp.full((own, 128), halo, jnp.int32),
        jnp.full((edge, 128), halo + strip, jnp.int32),
    ])
    places = tabs[...] + shift
    lanes = lax.broadcasted_iota(jnp.int32, places.shape, 1)
    width = strip + 2 * halo
    hits = [
        jnp.where(places == lanes + base, 1.0, 0.0).astype(jnp.bfloat16)
        for base in range(0, width, 128)
    ]
    hits = jnp.concatenate(hits, axis=1)
    spread_ref[...] = dot(hits, counts_ref[...], NN).astype(jnp.bfloat16)

    control_copy.wait()
    chunk = 256
    for base in range(0, members_here * levels, chunk):
        high, low = split_in_kernel(control_ref[base : base + chunk], 2)
        values = dot(spread_ref[...], high, NT) + dot(spread_ref[...], low, NT)
        partial[:, base : base + chunk] = SWEEP_SCALE * values

    start, wait = beside(
        partial.at[0:edge], partial.at[edge + own :],
        halo_in.at[0], halo_in.at[1], halo_send, halo_recv,
    )
    start()
    ensemble_copy.wait()
    own_hits = hits[edge : edge + own, halo : halo + strip]
    long = pair * state
    for i in range(pairs):
        picked[i] = dot(own_hits, ensemble_ref[i * long : (i + 1) * long], NT).astype(jnp.bfloat16)
    wait()

    nothing = jnp.zeros((own - edge, 128), jnp.float32)
    total = jnp.zeros((own, long), jnp.float32)
    for i in range(pairs):
        part = slice(i * 128, (i + 1) * 128)
        localized = (
            partial[edge : edge + own, part]
            + jnp.concatenate([halo_in[0, :, part], nothing])
            + jnp.concatenate([nothing, halo_in[1, :, part]])
        )
        spread_weights = dot(localized.astype(jnp.bfloat16), fold_ref[...], NN)
        total += spread_weights * picked[i].astype(jnp.float32)
    folded = total[:, :state]
    for i in range(1, pair):
        folded = folded + total[:, i * state : (i + 1) * state]
    folded = folded * scale
    sums[:, :state] = folded

    def rows_of(offset):
        peer = lax.rem(mem + offset, groups)
        return sums.at[pl.ds(pl.multiple_of(peer * slots, 8), slots)]

    copies = over_mem(rows_of, sums_in.at[mem], sum_send, sum_recv)
    sums_in[mem] = rows_of(0)[...]
    for copy in copies:
        copy.wait()
    block_sum = jnp.sum(sums_in[...], axis=0)[:, :state]
    block_sum = block_sum.astype(jnp.bfloat16).astype(jnp.float32)
    for t in range(tiles):
        rows_out[t, :, :state] = block_sum[t * cap : (t + 1) * cap]
    copies = over_tile(rows_out, rows_in, there_send, there_recv)
    rows_in[tile] = rows_out[tile]
    for copy in copies:
        copy.wait()
    for t in range(tiles):
        incoming[t * cap : (t + 1) * cap] = rows_in[t]

    model = dot(incoming[:, :state].astype(jnp.bfloat16), jacobian_ref[...], NT)
    channels = jacobian_ref.shape[0]
    observed = channel_ref.shape[1]
    channel_adjoint[...] = model

    def observe(row, carry):
        channel = channel_ref[pl.ds(row, 1)]
        ids = lax.broadcasted_iota(jnp.int32, (channels, observed), 0)
        found = jnp.where(ids == channel, 1.0, 0.0).astype(jnp.bfloat16)
        terms = split_in_kernel(channel_adjoint[pl.ds(row, 1)], 3)
        evolved = sum(dot(term, found, NN) for term in terms)
        left = jnp.where(
            filled_ref[pl.ds(row, 1)] > 0, evolved - innovation_ref[pl.ds(row, 1)], 0.0
        )
        departures_ref[pl.ds(row, 1)] = left
        terms = split_in_kernel(left * error_ref[pl.ds(row, 1)], 3)
        channel_adjoint[pl.ds(row, 1)] = sum(dot(term, found, NT) for term in terms)
        return carry

    lax.fori_loop(0, slots, observe, 0)
    column = dot(channel_adjoint[...].astype(jnp.bfloat16), jacobian_ref[...], NN)
    column = column.astype(jnp.bfloat16).astype(jnp.float32)
    for t in range(tiles):
        back_out[t, :, :state] = column[t * cap : (t + 1) * cap]
    copies = over_tile(back_out, back_in, back_send, back_recv)
    back_in[tile] = back_out[tile]
    for copy in copies:
        copy.wait()
    for t in range(tiles):
        adjoint[mem, t * cap : (t + 1) * cap] = back_in[t]
    for copy in over_mem(
        lambda offset: adjoint.at[mem], adjoint.at[mem], all_send, all_recv
    ):
        copy.wait()

    columns = jnp.concatenate([adjoint[k][:, :state] for k in range(groups)])
    columns = jnp.concatenate([columns] * pair, axis=1)
    for i in range(pairs):
        high, low = split_in_kernel(picked[i].astype(jnp.float32) * columns, 2)
        values = dot(high, fold_ref[...], NT) + dot(low, fold_ref[...], NT)
        extended_ref[edge : edge + own, i * 128 : (i + 1) * 128] = values * scale
    start, wait = beside(
        extended_ref.at[edge : 2 * edge], extended_ref.at[own : own + edge],
        extended_ref.at[0:edge], extended_ref.at[edge + own :], last_send, last_recv,
    )
    start()
    wait()


def body(
    control,
    ensemble,
    jacobian,
    send_columns,
    received_counts,
    observed_channel,
    innovation,
    error_weight,
):
    tiles = lax.axis_size("tile")
    groups = lax.axis_size("mem")
    tile_index = lax.axis_index("tile")
    members_here, levels, strip = control.shape
    variables = ensemble.shape[1]
    state = variables * levels
    scale = 1.0 / math.sqrt(members_here * groups)
    block = strip // groups
    owners, cap = send_columns.shape[1:]
    slots = owners * cap
    halo = SWEEPS * NY
    edge = -(-halo // block) * slots
    own = groups * slots
    rows = own + 2 * edge
    long = members_here * levels
    wide = -(-state // 128) * 128
    channels = jacobian.shape[0]
    observed = observed_channel.shape[-1]
    pair = 128 // levels

    offset = lax.axis_index("mem") * block
    table = jnp.broadcast_to(send_columns[0].reshape(slots, 1) + offset, (slots, 128))
    kinds = np.stack([
        sweep_counts(strip // NY, low, high).T for low in (False, True) for high in (False, True)
    ]).astype(jnp.bfloat16)
    kind = 2 * (tile_index == 0).astype(jnp.int32) + (tile_index == tiles - 1).astype(jnp.int32)
    counts = lax.dynamic_index_in_dim(jnp.asarray(kinds), kind, 0, keepdims=False)
    fold = np.arange(pair * levels)[:, None] == (
        np.arange(pair * state) // state * levels + np.arange(pair * state) % levels
    )
    filled = jnp.arange(cap, dtype=jnp.int32)[None, :, None] < received_counts[0][:, None, None]
    filled = jnp.broadcast_to(filled, (owners, cap, observed)).astype(jnp.int32)
    sizes = (tiles, groups, strip, block, owners, cap, edge, members_here, levels, variables, scale)
    f32, bf16 = jnp.float32, jnp.bfloat16
    vmem = pl.BlockSpec(memory_space=pltpu.VMEM)
    anywhere = pl.BlockSpec(memory_space=pl.ANY)
    dma = pltpu.SemaphoreType.DMA
    extended, spread, departures = pl.pallas_call(
        lambda *refs: kernel(sizes, *refs),
        out_shape=(
            jax.ShapeDtypeStruct((rows, long), f32),
            jax.ShapeDtypeStruct((rows, strip), bf16),
            jax.ShapeDtypeStruct((slots, observed), f32),
        ),
        in_specs=[vmem] * 8 + [anywhere] * 2,
        out_specs=(vmem, vmem, vmem),
        scratch_shapes=[
            pltpu.VMEM((long, strip), f32),
            pltpu.VMEM((long * variables, strip), bf16),
            pltpu.VMEM((rows, 128), jnp.int32),
            pltpu.VMEM((rows, long), f32),
            pltpu.VMEM((2, edge, long), f32),
            pltpu.VMEM((members_here // pair, own, pair * state), bf16),
            pltpu.VMEM((own, wide), f32),
            pltpu.VMEM((groups, slots, wide), f32),
            pltpu.VMEM((tiles, cap, wide), f32),
            pltpu.VMEM((tiles, cap, wide), f32),
            pltpu.VMEM((tiles, cap, wide), f32),
            pltpu.VMEM((tiles, cap, wide), f32),
            pltpu.VMEM((slots, wide), f32),
            pltpu.VMEM((slots, channels), f32),
            pltpu.VMEM((groups, slots, wide), f32),
            dma((2,)),
            dma((groups,)), dma((groups,)),
            dma((2,)), dma((2,)),
            dma((2,)), dma((2,)),
            dma((groups,)), dma((groups,)),
            dma((tiles,)), dma((tiles,)),
            dma((tiles,)), dma((tiles,)),
            dma((groups,)), dma((groups,)),
            dma((2,)), dma((2,)),
        ],
        compiler_params=pltpu.CompilerParams(
            collective_id=0, has_side_effects=True, vmem_limit_bytes=48 * 1024 * 1024
        ),
    )(
        table,
        counts,
        jnp.asarray(fold, bf16),
        jacobian,
        filled.reshape(slots, observed),
        observed_channel[0].reshape(slots, observed),
        innovation[0].reshape(slots, observed),
        error_weight[0].reshape(slots, observed),
        control.reshape(long, strip),
        ensemble.reshape(long * variables, strip),
    )
    high, low = split_two(extended)
    gradient = SWEEP_SCALE * (dot(high, spread, ((0,), (0,))) + dot(low, spread, ((0,), (0,))))
    departures = departures.reshape(1, owners, cap, observed)
    return (gradient.reshape(control.shape), departures)


def solution(mesh):
    in_specs = (
        P("mem", None, "tile"),
        P("mem", None, None, "tile"),
        P(),
        P(("tile", "mem"), None, None),
        P(("tile", "mem"), None),
        P(("tile", "mem"), None, None, None),
        P(("tile", "mem"), None, None, None),
        P(("tile", "mem"), None, None, None),
    )
    out_specs = (P("mem", None, "tile"), P(("tile", "mem"), None, None, None))
    return jax.shard_map(body, mesh=mesh, in_specs=in_specs, out_specs=out_specs, check_vma=False)
```

time: 135 us -> 58 us (0.43)
  blocking collectives: 52 us -> 0 us
  Pallas kernels: 0 us -> 49.6 us
  waiting for transfers between devices: 48.1 us -> 0 us
  matrix products: 12.1 us -> 2.24 us
  starting transfers between devices: 9.28 us -> 0 us
  other arithmetic: 7.24 us -> 0.84 us
    pallas_call x0 -> x1, Pallas kernels: none -> 49.6 us  [body(): pl.pallas_call(lambda *refs: kernel(sizes, *refs), out_shape=(jax.ShapeDt...]
    all_gather x1 -> x0, blocking collectives: 43 us -> none  [body(): tables = lax.all_gather(send_columns[0].reshape(slots), ('tile', 'mem'))]
    ppermute x4 -> x0, waiting for transfers between devices: 41.6 us -> none  [the longest x1 21 us: body(): from_left = lax.ppermute(partial[..., edge + own:], 'tile', forward)]
    dot_general x8 -> x2, matrix products: 12.1 us -> 2.24 us  [dot(): lax.dot_general(left, right, (dims, ((), ())), preferred_element_type=jnp...]
    all_to_all x1 -> x0, blocking collectives: 9.03 us -> none  [body(): lax.all_to_all(copies.reshape(owners * groups, cap, state), ('tile', 'mem...]
    all_to_all x1 -> x0, waiting for transfers between devices: 6.54 us -> none  [body(): lax.all_to_all(sums.reshape(owners * groups, cap, state), ('tile', 'mem')...]
    ppermute x4 -> x0, starting transfers between devices: 6.44 us -> none  [the longest x1 2.53 us: body(): low = lax.ppermute(member_adjoint[..., own - edge:], 'tile', forward)]
    reduce_sum x4 -> x0, other arithmetic: 3.65 us -> none  [the longest x1 1.69 us: body(): evolved = jnp.sum(jnp.where(found, model[:, None, :], 0.0), axis=2)]
  transfers between devices with their start and end apart: 5 -> 0, of which waited for: 3 -> 0; matrix products, arithmetic and copies ran while one was open for 2% -> 0% of each run, Pallas kernels for 0% -> 0%
where the time goes in v2:
time: 58 us; the launch traced here: 57.8 us
  Pallas kernels  49.6 us (86%)
  local copies, waits for them, and re-layouts  4.39 us (8%)
  matrix products  2.24 us (4%)
  other arithmetic  0.84 us (1%)
  between operations  0.75 us (1%)
    pallas_call x1, Pallas kernels, body(): pl.pallas_call(lambda *refs: kernel(sizes, *refs), out_shape=(jax.ShapeDt...  49.6 us
    dot_general x2, matrix products, dot(): lax.dot_general(left, right, (dims, ((), ())), preferred_element_type=jnp...  2.24 us
    unnamed x12, local copies, waits for them, and re-layouts  1.89 us
    squeeze x1, local copies, waits for them, and re-layouts, body(): lax.dynamic_index_in_dim(jnp.asarray(kinds), kind, 0, keepdims=False)  1.3 us

profile of v2, /device:TPU:0, one launch (start us, length us, event | category | flops | bytes accessed | tf_op | source)
XLA Modules:
  0.0 57.8 jit_solution(5093878243333048064)
XLA Ops:
  0.6 0.0 copy-start.1
  0.6 0.0 copy-start.4
  0.7 0.0 copy-start.3
  0.7 0.0 copy-start.2
  0.7 0.0 copy-start
  0.7 0.8 %broadcast_add_fusion = s32[1,8,2]{1,2,0:T(2,128)S(1)} fusion(s32[1,8,2]{1,2,0:T(2,128)} %param.13, s32[]{:T(128)S(6)} %mul.9), kind=kLoop, calls=%fused_computation.7 | loop fusion | flops 16 | bytes 132 | tf_op jit(solution)/shard_map/add | solution.py:371
  1.5 0.1 copy.14
  1.6 0.1 add.26
  1.7 0.7 %lt.33 = s32[8,2]{1,0:T(8,128)S(1)} broadcast(s32[8]{0:T(128)} %bitcast.21), dimensions={0} | broadcast | bytes 96 | tf_op jit(solution)/shard_map/lt | solution.py:380
  2.4 0.1 lt.34
  2.5 0.1 lt.31
  2.6 0.1 broadcast_in_dim.5.refs_4_
  2.7 0.1 broadcast_in_dim.4.refs_0_
  2.7 1.3 %copy.15.refs_3_ = bf16[640,320]{1,0:T(8,128)(2,1)S(1)} copy(bf16[640,320]{0,1:T(8,128)(2,1)} %param.12) | data formatting | bytes 819200 | tf_op args[2]
  4.0 1.3 %dynamic-slice_bitcast_fusion.refs_1_ = bf16[1024,512]{1,0:T(8,128)(2,1)S(1)} fusion(bf16[4,1024,512]{2,1,0:T(8,128)(2,1)} %constant.29.clone, s32[]{:T(128)S(6)} %select_n.4), kind=kLoop, calls=%fused_computation.1 | loop fusion | bytes 2097156 | tf_op jit(solution)/shard_map/jit(dynamic_index_in_dim)/squeeze | solution.py:376
  5.3 0.0 copy-done.1
  5.3 0.0 copy-done.4
  5.3 0.0 copy-done.3
  5.3 0.0 copy-done.2
  5.4 0.0 copy-done
  5.4 49.6 %shard_map.113 = (f32[128,1024]{1,0:T(8,128)S(1)}, bf16[128,512]{1,0:T(8,128)(2,1)S(1)}, f32[16,128]{1,0:T(8,128)S(1)}) custom-call(s32[16,128]{1,0:T(8,128)S(1)} %broadcast_in_dim.4.refs_0_, bf16[1024,512]{1,0:T(8,128)(2,1)S(1)} %dynamic-slice_bitcast_fusion.refs_1_, bf16[128,640]{1,0:T(8,128)(2,1)S(1)} %copy-done.1, bf16[640,320]{1,0:T(8,128)(2,1)S(1)} %copy.15.refs_3_, ...), custom_call_target="tpu_custom_call" | custom-call | tf_op jit(solution)/shard_map/pallas_call | solution.py:387
  54.9 0.5 fusion.2
  55.4 1.8 %add_multiply_fusion = f32[1024,512]{1,0:T(8,128)} fusion(f32[1024,512]{1,0:T(8,128)S(1)} %fusion.2, bf16[128,512]{1,0:T(8,128)(2,1)S(1)} %get-tuple-element.6, f32[128,1024]{1,0:T(8,128)S(1)} %get-tuple-element.5), kind=kOutput, calls=%fused_computation | convolution fusion | flops 135659520 | bytes 4849664 | tf_op jit(solution)/shard_map/dot_general | solution.py:49
  57.2 0.6 %copy.17 = f32[1,8,2,128]{3,2,1,0:T(2,128)} copy(f32[1,8,2,128]{3,2,1,0:T(2,128)S(1)} %bitcast.15) | data formatting | bytes 16384
  (2 shorter events, 0.0 us)
Async XLA Ops:
  0.6 4.7 %copy-start.1 = (bf16[128,640]{1,0:T(8,128)(2,1)S(1)}, bf16[128,640]{1,0:T(8,128)(2,1)}, u32[]{:S(2)}) copy-start(bf16[128,640]{1,0:T(8,128)(2,1)} %constant.30.clone.refs_2_) | copy-start | bytes 491524
  0.6 4.7 %copy-start.4 = (f32[1,8,2,128]{3,2,1,0:T(2,128)S(1)}, f32[1,8,2,128]{3,2,1,0:T(2,128)}, u32[]{:S(2)}) copy-start(f32[1,8,2,128]{3,2,1,0:T(2,128)} %param.17) | copy-start | bytes 24580
  0.7 4.7 %copy-start.3 = (f32[1,8,2,128]{3,2,1,0:T(2,128)S(1)}, f32[1,8,2,128]{3,2,1,0:T(2,128)}, u32[]{:S(2)}) copy-start(f32[1,8,2,128]{3,2,1,0:T(2,128)} %param.16) | copy-start | bytes 24580
  0.7 4.7 %copy-start.2 = (s32[1,8,2,128]{3,2,1,0:T(2,128)S(1)}, s32[1,8,2,128]{3,2,1,0:T(2,128)}, u32[]{:S(2)}) copy-start(s32[1,8,2,128]{3,2,1,0:T(2,128)} %param.15) | copy-start | bytes 24580
  0.7 4.7 %copy-start = (f32[16,64,512]{2,1,0:T(8,128)S(1)}, f32[16,64,512]{2,1,0:T(8,128)}, u32[]{:S(2)}) copy-start(f32[16,64,512]{2,1,0:T(8,128)} %param.10) | copy-start | bytes 6291460

commit v3 on v2

--- a/solution.py
+++ b/solution.py
@@ -31,11 +31,6 @@
     return field.reshape(strip_rows * NY, rows * NY)
 
 
-def split_two(values):
-    high = lax.reduce_precision(values, 8, 7)
-    return high.astype(jnp.bfloat16), (values - high).astype(jnp.bfloat16)
-
-
 def split_in_kernel(values, terms):
     pieces = []
     for _ in range(terms):
@@ -56,22 +51,25 @@
 def kernel(
     sizes,
     table_ref,
-    counts_ref,
     fold_ref,
-    jacobian_ref,
-    filled_ref,
     channel_ref,
     innovation_ref,
     error_ref,
     control_hbm,
     ensemble_hbm,
+    counts_hbm,
+    jacobian_hbm,
     extended_ref,
     spread_ref,
     departures_ref,
     control_ref,
     ensemble_ref,
+    counts_ref,
+    jacobian_ref,
+    found_ref,
     tabs,
     partial,
+    halo_out,
     halo_in,
     picked,
     sums,
@@ -113,8 +111,13 @@
 
     control_copy = pltpu.make_async_copy(control_hbm, control_ref, local_sem.at[0])
     ensemble_copy = pltpu.make_async_copy(ensemble_hbm, ensemble_ref, local_sem.at[1])
+    kind = jnp.where(tile == 0, 2, 0) + jnp.where(tile == tiles - 1, 1, 0)
+    counts_copy = pltpu.make_async_copy(counts_hbm.at[kind], counts_ref, local_sem.at[2])
+    jacobian_copy = pltpu.make_async_copy(jacobian_hbm, jacobian_ref, local_sem.at[3])
+    counts_copy.start()
     control_copy.start()
     ensemble_copy.start()
+    jacobian_copy.start()
 
     def to_mem(offset):
         return {"tile": tile, "mem": lax.rem(mem + offset, groups)}
@@ -195,19 +198,19 @@
         return copies
 
     my_rows = tabs.at[pl.ds(pl.multiple_of(edge + mem * slots, 8), slots)]
-    my_rows[...] = table_ref[...]
+    my_rows[...] = table_ref[0:slots]
 
     @pl.when(tile == 0)
     def _():
         tabs[0:edge] = jnp.full((edge, 128), -8 * strip, jnp.int32)
         halo_in[0] = jnp.zeros_like(halo_in[0])
-        extended_ref[0:edge] = jnp.zeros((edge, members_here * levels), jnp.float32)
+        extended_ref[0:edge] = jnp.zeros((edge, members_here * levels), jnp.bfloat16)
 
     @pl.when(tile == tiles - 1)
     def _():
         tabs[edge + own :] = jnp.full((edge, 128), 8 * strip, jnp.int32)
         halo_in[1] = jnp.zeros_like(halo_in[1])
-        extended_ref[edge + own :] = jnp.zeros((edge, members_here * levels), jnp.float32)
+        extended_ref[edge + own :] = jnp.zeros((edge, members_here * levels), jnp.bfloat16)
 
     for copy in over_mem(lambda offset: my_rows, my_rows, table_send, table_recv):
         copy.wait()
@@ -231,6 +234,7 @@
         for base in range(0, width, 128)
     ]
     hits = jnp.concatenate(hits, axis=1)
+    counts_copy.wait()
     spread_ref[...] = dot(hits, counts_ref[...], NN).astype(jnp.bfloat16)
 
     control_copy.wait()
@@ -240,8 +244,10 @@
         values = dot(spread_ref[...], high, NT) + dot(spread_ref[...], low, NT)
         partial[:, base : base + chunk] = SWEEP_SCALE * values
 
+    halo_out[0] = partial[0:edge].astype(jnp.bfloat16)
+    halo_out[1] = partial[edge + own :].astype(jnp.bfloat16)
     start, wait = beside(
-        partial.at[0:edge], partial.at[edge + own :],
+        halo_out.at[0], halo_out.at[1],
         halo_in.at[0], halo_in.at[1], halo_send, halo_recv,
     )
     start()
@@ -250,6 +256,17 @@
     long = pair * state
     for i in range(pairs):
         picked[i] = dot(own_hits, ensemble_ref[i * long : (i + 1) * long], NT).astype(jnp.bfloat16)
+    channels = jacobian_ref.shape[1]
+    observed = channel_ref.shape[1]
+
+    def find(row, carry):
+        ids = lax.broadcasted_iota(jnp.int32, (channels, observed), 0)
+        hit = ids == channel_ref[pl.ds(row, 1)]
+        found_ref[row] = jnp.where(hit, 1.0, 0.0).astype(jnp.bfloat16)
+        return carry
+
+    lax.fori_loop(0, slots, find, 0)
+    jacobian_copy.wait()
     wait()
 
     nothing = jnp.zeros((own - edge, 128), jnp.float32)
@@ -258,8 +275,8 @@
         part = slice(i * 128, (i + 1) * 128)
         localized = (
             partial[edge : edge + own, part]
-            + jnp.concatenate([halo_in[0, :, part], nothing])
-            + jnp.concatenate([nothing, halo_in[1, :, part]])
+            + jnp.concatenate([halo_in[0, :, part].astype(jnp.float32), nothing])
+            + jnp.concatenate([nothing, halo_in[1, :, part].astype(jnp.float32)])
         )
         spread_weights = dot(localized.astype(jnp.bfloat16), fold_ref[...], NN)
         total += spread_weights * picked[i].astype(jnp.float32)
@@ -288,27 +305,28 @@
     for t in range(tiles):
         incoming[t * cap : (t + 1) * cap] = rows_in[t]
 
-    model = dot(incoming[:, :state].astype(jnp.bfloat16), jacobian_ref[...], NT)
-    channels = jacobian_ref.shape[0]
-    observed = channel_ref.shape[1]
+    model = dot(incoming[:, :state].astype(jnp.bfloat16), jacobian_ref[...], NN)
     channel_adjoint[...] = model
 
+    def stacked(values):
+        terms = [term.astype(jnp.float32) for term in split_in_kernel(values, 3)]
+        blank = jnp.zeros((5, values.shape[1]), jnp.float32)
+        return jnp.concatenate(terms + [blank]).astype(jnp.bfloat16)
+
     def observe(row, carry):
-        channel = channel_ref[pl.ds(row, 1)]
-        ids = lax.broadcasted_iota(jnp.int32, (channels, observed), 0)
-        found = jnp.where(ids == channel, 1.0, 0.0).astype(jnp.bfloat16)
-        terms = split_in_kernel(channel_adjoint[pl.ds(row, 1)], 3)
-        evolved = sum(dot(term, found, NN) for term in terms)
+        found = found_ref[row]
+        evolved = dot(stacked(channel_adjoint[pl.ds(row, 1)]), found, NN)
+        evolved = jnp.sum(evolved, axis=0, keepdims=True)
         left = jnp.where(
-            filled_ref[pl.ds(row, 1)] > 0, evolved - innovation_ref[pl.ds(row, 1)], 0.0
+            table_ref[pl.ds(slots + row, 1)] > 0, evolved - innovation_ref[pl.ds(row, 1)], 0.0
         )
         departures_ref[pl.ds(row, 1)] = left
-        terms = split_in_kernel(left * error_ref[pl.ds(row, 1)], 3)
-        channel_adjoint[pl.ds(row, 1)] = sum(dot(term, found, NT) for term in terms)
+        adjoint_terms = dot(stacked(left * error_ref[pl.ds(row, 1)]), found, NT)
+        channel_adjoint[pl.ds(row, 1)] = jnp.sum(adjoint_terms, axis=0, keepdims=True)
         return carry
 
-    lax.fori_loop(0, slots, observe, 0)
-    column = dot(channel_adjoint[...].astype(jnp.bfloat16), jacobian_ref[...], NN)
+    lax.fori_loop(0, slots, observe, 0, unroll=math.gcd(slots, 16))
+    column = dot(channel_adjoint[...].astype(jnp.bfloat16), jacobian_ref[...], NT)
     column = column.astype(jnp.bfloat16).astype(jnp.float32)
     for t in range(tiles):
         back_out[t, :, :state] = column[t * cap : (t + 1) * cap]
@@ -328,7 +346,7 @@
     for i in range(pairs):
         high, low = split_in_kernel(picked[i].astype(jnp.float32) * columns, 2)
         values = dot(high, fold_ref[...], NT) + dot(low, fold_ref[...], NT)
-        extended_ref[edge : edge + own, i * 128 : (i + 1) * 128] = values * scale
+        extended_ref[edge : edge + own, i * 128 : (i + 1) * 128] = (values * scale).astype(jnp.bfloat16)
     start, wait = beside(
         extended_ref.at[edge : 2 * edge], extended_ref.at[own : own + edge],
         extended_ref.at[0:edge], extended_ref.at[edge + own :], last_send, last_recv,
@@ -349,7 +367,6 @@
 ):
     tiles = lax.axis_size("tile")
     groups = lax.axis_size("mem")
-    tile_index = lax.axis_index("tile")
     members_here, levels, strip = control.shape
     variables = ensemble.shape[1]
     state = variables * levels
@@ -372,13 +389,12 @@
     kinds = np.stack([
         sweep_counts(strip // NY, low, high).T for low in (False, True) for high in (False, True)
     ]).astype(jnp.bfloat16)
-    kind = 2 * (tile_index == 0).astype(jnp.int32) + (tile_index == tiles - 1).astype(jnp.int32)
-    counts = lax.dynamic_index_in_dim(jnp.asarray(kinds), kind, 0, keepdims=False)
     fold = np.arange(pair * levels)[:, None] == (
         np.arange(pair * state) // state * levels + np.arange(pair * state) % levels
     )
     filled = jnp.arange(cap, dtype=jnp.int32)[None, :, None] < received_counts[0][:, None, None]
-    filled = jnp.broadcast_to(filled, (owners, cap, observed)).astype(jnp.int32)
+    filled = jnp.broadcast_to(filled, (owners, cap, 128)).astype(jnp.int32)
+    table = jnp.concatenate([table, filled.reshape(slots, 128)])
     sizes = (tiles, groups, strip, block, owners, cap, edge, members_here, levels, variables, scale)
     f32, bf16 = jnp.float32, jnp.bfloat16
     vmem = pl.BlockSpec(memory_space=pltpu.VMEM)
@@ -387,18 +403,22 @@
     extended, spread, departures = pl.pallas_call(
         lambda *refs: kernel(sizes, *refs),
         out_shape=(
-            jax.ShapeDtypeStruct((rows, long), f32),
+            jax.ShapeDtypeStruct((rows, long), bf16),
             jax.ShapeDtypeStruct((rows, strip), bf16),
             jax.ShapeDtypeStruct((slots, observed), f32),
         ),
-        in_specs=[vmem] * 8 + [anywhere] * 2,
+        in_specs=[vmem] * 5 + [anywhere] * 4,
         out_specs=(vmem, vmem, vmem),
         scratch_shapes=[
             pltpu.VMEM((long, strip), f32),
             pltpu.VMEM((long * variables, strip), bf16),
+            pltpu.VMEM(kinds.shape[1:], bf16),
+            pltpu.VMEM((state, channels), bf16),
+            pltpu.VMEM((slots, channels, observed), bf16),
             pltpu.VMEM((rows, 128), jnp.int32),
             pltpu.VMEM((rows, long), f32),
-            pltpu.VMEM((2, edge, long), f32),
+            pltpu.VMEM((2, edge, long), bf16),
+            pltpu.VMEM((2, edge, long), bf16),
             pltpu.VMEM((members_here // pair, own, pair * state), bf16),
             pltpu.VMEM((own, wide), f32),
             pltpu.VMEM((groups, slots, wide), f32),
@@ -409,7 +429,7 @@
             pltpu.VMEM((slots, wide), f32),
             pltpu.VMEM((slots, channels), f32),
             pltpu.VMEM((groups, slots, wide), f32),
-            dma((2,)),
+            dma((4,)),
             dma((groups,)), dma((groups,)),
             dma((2,)), dma((2,)),
             dma((2,)), dma((2,)),
@@ -424,18 +444,16 @@
         ),
     )(
         table,
-        counts,
         jnp.asarray(fold, bf16),
-        jacobian,
-        filled.reshape(slots, observed),
         observed_channel[0].reshape(slots, observed),
         innovation[0].reshape(slots, observed),
         error_weight[0].reshape(slots, observed),
         control.reshape(long, strip),
         ensemble.reshape(long * variables, strip),
-    )
-    high, low = split_two(extended)
-    gradient = SWEEP_SCALE * (dot(high, spread, ((0,), (0,))) + dot(low, spread, ((0,), (0,))))
+        jnp.asarray(kinds),
+        jnp.transpose(jacobian),
+    )
+    gradient = SWEEP_SCALE * dot(extended, spread, ((0,), (0,)))
     departures = departures.reshape(1, owners, cap, observed)
     return (gradient.reshape(control.shape), departures)
 

time: 58 us -> 51 us (0.88)
  Pallas kernels: 49.6 us -> 40.1 us
  local copies, waits for them, and re-layouts: 4.39 us -> 7.33 us
    pallas_call x1, Pallas kernels: 49.6 us -> 40.1 us  [body(): pl.pallas_call(lambda *refs: kernel(sizes, *refs), out_shape=(jax.ShapeDt...]
    unnamed x12 -> x13, local copies, waits for them, and re-layouts: 1.89 us -> 6.2 us
    squeeze x1 -> x0, local copies, waits for them, and re-layouts: 1.3 us -> none  [body(): lax.dynamic_index_in_dim(jnp.asarray(kinds), kind, 0, keepdims=False)]
    dot_general x2 -> x1, matrix products: 2.24 us -> 1.77 us  [dot(): lax.dot_general(left, right, (dims, ((), ())), preferred_element_type=jnp...]
where the time goes in v3:
time: 51 us; the launch traced here: 50.6 us
  Pallas kernels  40.1 us (79%)
  local copies, waits for them, and re-layouts  7.33 us (14%)
  matrix products  1.77 us (3%)
  other arithmetic  0.77 us (2%)
  between operations  0.65 us (1%)
    pallas_call x1, Pallas kernels, body(): pl.pallas_call(lambda *refs: kernel(sizes, *refs), out_shape=(jax.ShapeDt...  40.1 us
    unnamed x13, local copies, waits for them, and re-layouts  6.2 us
    dot_general x1, matrix products, dot(): lax.dot_general(left, right, (dims, ((), ())), preferred_element_type=jnp...  1.77 us

profile of v3, /device:TPU:0, one launch (start us, length us, event | category | flops | bytes accessed | tf_op | source)
XLA Modules:
  0.0 50.6 jit_solution(14622280058021538001)
XLA Ops:
  0.6 0.7 %broadcast_add_fusion = s32[1,8,2]{1,2,0:T(2,128)S(1)} fusion(s32[1,8,2]{1,2,0:T(2,128)} %param.13, s32[]{:T(128)S(6)} %mul.9), kind=kLoop, calls=%fused_computation.3 | loop fusion | flops 16 | bytes 132 | tf_op jit(solution)/shard_map/add | solution.py:388
  1.3 0.1 copy.13
  1.4 0.1 reshape.56
  1.5 0.7 %lt.28 = s32[8,2]{1,0:T(8,128)S(1)} broadcast(s32[8]{0:T(128)} %bitcast.21), dimensions={0} | broadcast | bytes 96 | tf_op jit(solution)/shard_map/lt | solution.py:395
  2.2 0.1 lt.29
  2.3 0.1 lt.26
  2.4 0.1 pad_add_fusion
  2.5 0.1 broadcast.25.refs_0_
  2.5 0.0 copy-start
  2.5 1.6 %copy-done = f32[16,64,512]{2,1,0:T(8,128)S(1)} copy-done((f32[16,64,512]{2,1,0:T(8,128)S(1)}, f32[16,64,512]{2,1,0:T(8,128)}, u32[]{:S(2)}) %copy-start) | copy-done | bytes 2097176
  4.1 0.0 copy-start.1
  4.1 1.0 %copy-done.1 = bf16[640,320]{0,1:T(8,128)(2,1)S(1)} copy-done((bf16[640,320]{0,1:T(8,128)(2,1)S(1)}, bf16[640,320]{0,1:T(8,128)(2,1)}, u32[]{:S(2)}) %copy-start.1) | copy-done | bytes 409624
  5.1 0.0 copy-start.2
  5.1 0.9 %copy-done.2 = bf16[128,640]{1,0:T(8,128)(2,1)S(1)} copy-done((bf16[128,640]{1,0:T(8,128)(2,1)S(1)}, bf16[128,640]{1,0:T(8,128)(2,1)}, u32[]{:S(2)}) %copy-start.2) | copy-done | bytes 163864
  6.1 0.0 copy-start.3
  6.1 0.7 %copy-done.3 = s32[1,8,2,128]{3,2,1,0:T(2,128)S(1)} copy-done((s32[1,8,2,128]{3,2,1,0:T(2,128)S(1)}, s32[1,8,2,128]{3,2,1,0:T(2,128)}, u32[]{:S(2)}) %copy-start.3) | copy-done | bytes 8216
  6.8 0.0 copy-start.4
  6.8 0.7 %copy-done.4 = f32[1,8,2,128]{3,2,1,0:T(2,128)S(1)} copy-done((f32[1,8,2,128]{3,2,1,0:T(2,128)S(1)}, f32[1,8,2,128]{3,2,1,0:T(2,128)}, u32[]{:S(2)}) %copy-start.4) | copy-done | bytes 8216
  7.4 0.0 copy-start.5
  7.5 0.7 %copy-done.5 = f32[1,8,2,128]{3,2,1,0:T(2,128)S(1)} copy-done((f32[1,8,2,128]{3,2,1,0:T(2,128)S(1)}, f32[1,8,2,128]{3,2,1,0:T(2,128)}, u32[]{:S(2)}) %copy-start.5) | copy-done | bytes 8216
  8.1 40.1 %shard_map.113 = (bf16[128,1024]{1,0:T(8,128)(2,1)S(1)}, bf16[128,512]{1,0:T(8,128)(2,1)S(1)}, f32[16,128]{1,0:T(8,128)S(1)}) custom-call(s32[32,128]{1,0:T(8,128)S(1)} %broadcast.25.refs_0_, bf16[128,640]{1,0:T(8,128)(2,1)S(1)} %copy-done.2, s32[16,128]{1,0:T(8,128)S(1)} %bitcast.16, f32[16,128]{1,0:T(8,128)S(1)} %bitcast.17, f32[16,128]{1,0:T(8,128)S(1)} %bitcast.18, ...), custom_call_target="tpu_custom_call" | custom-call | tf_op jit(solution)/shard_map/pallas_call | solution.py:403
  48.2 1.8 %convolution_multiply_fusion = f32[1024,512]{1,0:T(8,128)} fusion(bf16[128,1024]{1,0:T(8,128)(2,1)S(1)} %get-tuple-element.5, bf16[128,512]{1,0:T(8,128)(2,1)S(1)} %get-tuple-element.6), kind=kOutput, calls=%fused_computation | convolution fusion | flops 134742016 | bytes 2490368 | tf_op jit(solution)/shard_map/dot_general | solution.py:44
  50.0 0.6 %copy.15 = f32[1,8,2,128]{3,2,1,0:T(2,128)} copy(f32[1,8,2,128]{3,2,1,0:T(2,128)S(1)} %bitcast.15) | data formatting | bytes 16384
  (2 shorter events, 0.0 us)
Async XLA Ops:
  2.5 1.6 %copy-start = (f32[16,64,512]{2,1,0:T(8,128)S(1)}, f32[16,64,512]{2,1,0:T(8,128)}, u32[]{:S(2)}) copy-start(f32[16,64,512]{2,1,0:T(8,128)} %param.10) | copy-start | bytes 6291460
  4.1 1.0 %copy-start.1 = (bf16[640,320]{0,1:T(8,128)(2,1)S(1)}, bf16[640,320]{0,1:T(8,128)(2,1)}, u32[]{:S(2)}) copy-start(bf16[640,320]{0,1:T(8,128)(2,1)} %param.12) | copy-start | bytes 1228804
  5.1 0.9 %copy-start.2 = (bf16[128,640]{1,0:T(8,128)(2,1)S(1)}, bf16[128,640]{1,0:T(8,128)(2,1)}, u32[]{:S(2)}) copy-start(bf16[128,640]{1,0:T(8,128)(2,1)} %constant.12.clone.refs_1_) | copy-start | bytes 491524
  6.1 0.7 %copy-start.3 = (s32[1,8,2,128]{3,2,1,0:T(2,128)S(1)}, s32[1,8,2,128]{3,2,1,0:T(2,128)}, u32[]{:S(2)}) copy-start(s32[1,8,2,128]{3,2,1,0:T(2,128)} %param.15) | copy-start | bytes 24580
  6.8 0.7 %copy-start.4 = (f32[1,8,2,128]{3,2,1,0:T(2,128)S(1)}, f32[1,8,2,128]{3,2,1,0:T(2,128)}, u32[]{:S(2)}) copy-start(f32[1,8,2,128]{3,2,1,0:T(2,128)} %param.16) | copy-start | bytes 24580
  7.4 0.7 %copy-start.5 = (f32[1,8,2,128]{3,2,1,0:T(2,128)S(1)}, f32[1,8,2,128]{3,2,1,0:T(2,128)}, u32[]{:S(2)}) copy-start(f32[1,8,2,128]{3,2,1,0:T(2,128)} %param.17) | copy-start | bytes 24580
